TPU v7x, 128 devices: a whole 4x4x4 slice. The times are simulated.
128 devices in a mesh: dp: 64 (over x, z_hi, y, core), tensor: 2 (over z_lo).
Axes of the slice: x: 4, y: 4, z: 4 (z_hi: 2, z_lo: 2; z = z_hi * 2 + z_lo), core: 2. Of those that a mesh axis runs over, the one named last changes fastest.
Arguments:
- hidden: bfloat16 [32768, 1536], P(('dp', 'tensor')), may hold values from -24 to 24
- segments: int32 [64, 512], P('dp'), may hold values from 0 to 3, never falling along the last dimension, each value on 1 to 384 neighbouring positions
- norm_gain: float32 [1536], replicated, may hold values from 0.5 to 1.5
- in_weight: bfloat16 [2, 1536, 3072], P(None, 'dp', 'tensor'), may hold values from -0.15625 to 0.15625
- bc_weight: bfloat16 [1536, 256], P('dp'), may hold values from -0.15625 to 0.15625
- step_weight: bfloat16 [1536, 48], P('dp', 'tensor'), may hold values from -0.15625 to 0.15625
- conv_weight: float32 [4, 3328], replicated, may hold values from -3 to 3
- conv_bias: float32 [3328], replicated, may hold values from -1.2 to 1.2
- step_bias: float32 [48], replicated, may hold values from -6 to -2
- decay_log: float32 [48], replicated, may hold values from 0 to 2.77
- skip_gain: float32 [48], replicated, may hold values from 0.1 to 1.9
- gate_gain: float32 [3072], replicated, may hold values from 0.5 to 1.5
- out_weight: bfloat16 [3072, 1536], P('tensor', 'dp'), may hold values from -0.109375 to 0.109375
- cotangent: bfloat16 [32768, 1536], P(('dp', 'tensor')), may hold values from -24 to 24
Outputs:
- mixed: bfloat16 [32768, 1536], P(('dp', 'tensor'))
- grad_hidden: float32 [32768, 1536], P(('dp', 'tensor'))
- grad_norm_gain: float32 [1536], replicated
- grad_in_weight: float32 [2, 1536, 3072], P(None, 'dp', 'tensor')
- grad_bc_weight: float32 [1536, 256], P('dp')
- grad_step_weight: float32 [1536, 48], P('dp', 'tensor')
- grad_conv_weight: float32 [4, 3328], replicated
- grad_conv_bias: float32 [3328], replicated
- grad_step_bias: float32 [48], replicated
- grad_decay_log: float32 [48], replicated
- grad_skip_gain: float32 [48], replicated
- grad_gate_gain: float32 [3072], replicated
- grad_out_weight: float32 [3072, 1536], P('tensor', 'dp')
Inputs may be any that keep to these rules, and one draw needn't show every extreme that they name: `segments`: in each row, the 512 tokens of one pack, segment numbers never fall; 4 documents of 1 to 384 tokens each, one of exactly 384.
All inputs are finite; a program needn't handle non-finite values.
Results may differ from a plain program's by a relative error of at most 0.011.
Values may be sent and summed in bfloat16 or wider, within the bound.
No kernel may reach another device: no remote copies, remote signals or barrier semaphores. Data moves between devices by JAX's collectives and lax.ppermute only.
A program may use at most 128 MiB of HBM per device.

v0:
```python
import jax
import jax.numpy as jnp
from jax import lax
from jax.sharding import PartitionSpec as P

EPS = 1e-05


def silu_slope(values):
    sigmoid_v = jax.nn.sigmoid(values)
    return sigmoid_v * (1.0 + values * (1.0 - sigmoid_v))


def shift_down(values, offset):
    if offset == 0:
        return values
    return jnp.pad(values, ((offset, 0), (0, 0)))[: values.shape[0]]


def shift_up(values, offset):
    if offset == 0:
        return values
    return jnp.pad(values, ((0, offset), (0, 0)))[offset:]


def seg_masks(seg_row, kernel):
    masks_out = []
    for tap_index in range(kernel):
        offset = kernel - 1 - tap_index
        earlier = jnp.pad(seg_row, (offset, 0), constant_values=-1)[: seg_row.shape[0]]
        masks_out.append((earlier == seg_row).astype(jnp.float32))
    return masks_out


def contract_rows(left, right):
    return lax.dot_general(
        left, right, (((0,), (0,)), ((), ())), preferred_element_type=jnp.float32
    )


def contract_cols(left, right):
    return lax.dot_general(
        left, right, (((1,), (1,)), ((), ())), preferred_element_type=jnp.float32
    )


def decay_parts(visible, visible_f, sum_head, step_head):
    log_decay = sum_head[:, None] - sum_head[None, :]
    decay_mat = jnp.exp(jnp.where(visible, log_decay, 0.0)) * visible_f
    return (decay_mat, decay_mat * step_head[None, :])


def on_device(
    hidden,
    segments,
    norm_gain,
    in_weight,
    bc_weight,
    step_weight,
    conv_weight,
    conv_bias,
    step_bias,
    decay_log,
    skip_gain,
    gate_gain,
    out_weight,
    cotangent,
):
    tensor_pos = lax.axis_index("tensor")
    tensor_count = lax.axis_size("tensor")
    tok_rows, model_width = hidden.shape
    inner_local = in_weight.shape[2]
    heads_local = step_weight.shape[1]
    inner_total = inner_local * tensor_count
    head_count = heads_local * tensor_count
    head_size = inner_local // heads_local
    state_size = bc_weight.shape[1] // 2
    kernel = conv_weight.shape[0]
    seg_row = segments[0]
    length = seg_row.shape[0]
    inner_start = tensor_pos * inner_local
    head_start = tensor_pos * heads_local
    full_in, full_bc, full_step, full_out = (
        lax.all_gather(in_weight, "dp", axis=1, tiled=True),
        lax.all_gather(bc_weight, "dp", axis=0, tiled=True),
        lax.all_gather(step_weight, "dp", axis=0, tiled=True),
        lax.all_gather(out_weight, "dp", axis=1, tiled=True),
    )
    resid = hidden.astype(jnp.float32)
    norm_scale = lax.rsqrt(jnp.mean(resid * resid, axis=-1, keepdims=True) + EPS)
    normed = (resid * norm_scale * norm_gain).astype(jnp.bfloat16)
    normed_all = lax.all_gather(normed, "tensor", axis=0, tiled=True)
    gate_pre = jnp.dot(normed_all, full_in[0], preferred_element_type=jnp.float32)
    inner_pre = jnp.dot(normed_all, full_in[1], preferred_element_type=jnp.float32)
    bc_pre = jnp.dot(normed_all, full_bc, preferred_element_type=jnp.float32)
    step_pre = jnp.dot(
        normed_all, full_step, preferred_element_type=jnp.float32
    ) + lax.dynamic_slice_in_dim(step_bias, head_start, heads_local)
    conv_local = jnp.concatenate(
        [
            lax.dynamic_slice_in_dim(conv_weight, inner_start, inner_local, 1),
            conv_weight[:, inner_total:],
        ],
        axis=1,
    )
    bias_local = jnp.concatenate(
        [lax.dynamic_slice_in_dim(conv_bias, inner_start, inner_local, 0), conv_bias[inner_total:]]
    )
    channels = jnp.concatenate([inner_pre, bc_pre], axis=1)
    conv_masks = seg_masks(seg_row, kernel)
    conv_out = bias_local
    for tap_index in range(kernel):
        offset = kernel - 1 - tap_index
        conv_out = (
            conv_out
            + conv_local[tap_index] * shift_down(channels, offset) * conv_masks[tap_index][:, None]
        )
    activated = jax.nn.silu(conv_out)
    inner_act = activated[:, :inner_local].astype(jnp.bfloat16)
    b_proj = activated[:, inner_local : inner_local + state_size].astype(jnp.bfloat16)
    c_proj = activated[:, inner_local + state_size :].astype(jnp.bfloat16)
    step_size = jax.nn.softplus(step_pre)
    decay_rate = -jnp.exp(lax.dynamic_slice_in_dim(decay_log, head_start, heads_local))
    decay_sum = jnp.cumsum(step_size * decay_rate, axis=0)
    positions = jnp.arange(length)
    visible = (positions[:, None] >= positions[None, :]) & (seg_row[:, None] == seg_row[None, :])
    visible_f = visible.astype(jnp.float32)
    scores = contract_cols(c_proj, b_proj)
    act_heads = inner_act.reshape(length, heads_local, head_size).transpose(1, 0, 2)

    def mix_head(carry, pieces):
        sum_head, step_head, act_head = pieces
        decay_mat, decay_dt = decay_parts(visible, visible_f, sum_head, step_head)
        weights = (scores * decay_dt).astype(jnp.bfloat16)
        return (carry, jnp.dot(weights, act_head, preferred_element_type=jnp.float32))

    unused, mixed_heads = lax.scan(
        mix_head, jnp.zeros((), jnp.float32), (decay_sum.T, step_size.T, act_heads)
    )
    skip_cols = jnp.repeat(lax.dynamic_slice_in_dim(skip_gain, head_start, heads_local), head_size)
    inner_f = inner_act.astype(jnp.float32)
    mixer_y = mixed_heads.transpose(1, 0, 2).reshape(length, inner_local) + skip_cols * inner_f
    gate_act = jax.nn.silu(gate_pre)
    gated = mixer_y * gate_act
    square_sum = lax.psum(jnp.sum(gated * gated, axis=-1), "tensor")
    gate_scale = lax.rsqrt(square_sum / inner_total + EPS)[:, None]
    gain_local = lax.dynamic_slice_in_dim(gate_gain, inner_start, inner_local)
    gnormed = (gated * gate_scale * gain_local).astype(jnp.bfloat16)
    branch = lax.psum_scatter(
        jnp.dot(gnormed, full_out, preferred_element_type=jnp.float32).astype(jnp.bfloat16),
        "tensor",
        scatter_dimension=0,
        tiled=True,
    ).astype(jnp.float32)
    mixed = (resid + branch).astype(jnp.bfloat16)
    cot_all = lax.all_gather(cotangent, "tensor", axis=0, tiled=True)
    back_in, back_bc, back_step, back_out = (
        lax.all_gather(in_weight, "dp", axis=1, tiled=True),
        lax.all_gather(bc_weight, "dp", axis=0, tiled=True),
        lax.all_gather(step_weight, "dp", axis=0, tiled=True),
        lax.all_gather(out_weight, "dp", axis=1, tiled=True),
    )
    grad_gn = contract_cols(cot_all, back_out)
    grad_w_out = contract_rows(gnormed, cot_all)
    norm_stat = lax.psum(jnp.sum(grad_gn * gain_local * gated, axis=-1), "tensor")
    grad_gated = (
        gate_scale * gain_local * grad_gn
        - gated * gate_scale**3 * (norm_stat / inner_total)[:, None]
    )
    grad_gain_local = jnp.sum(grad_gn * gated * gate_scale, axis=0)
    grad_y = grad_gated * gate_act
    grad_gate = grad_gated * mixer_y * silu_slope(gate_pre)
    grad_skip_local = jnp.sum(
        (grad_y * inner_f).reshape(length, heads_local, head_size), axis=(0, 2)
    )
    dy_heads = (
        grad_y.astype(jnp.bfloat16).reshape(length, heads_local, head_size).transpose(1, 0, 2)
    )

    def back_head(score_acc, pieces):
        sum_head, step_head, act_head, dy_head = pieces
        decay_mat, decay_dt = decay_parts(visible, visible_f, sum_head, step_head)
        weights = (scores * decay_dt).astype(jnp.bfloat16)
        grad_weights = contract_cols(dy_head, act_head)
        grad_head = contract_rows(weights, dy_head)
        grad_decay = grad_weights * scores
        flowed = grad_decay * decay_dt
        grad_sum = jnp.sum(flowed, axis=1) - jnp.sum(flowed, axis=0)
        grad_step = jnp.sum(grad_decay * decay_mat, axis=0)
        return (score_acc + grad_weights * decay_dt, (grad_head, grad_sum, grad_step))

    score_part, (grad_heads, grad_sums, grad_steps) = lax.scan(
        back_head,
        jnp.zeros((length, length), jnp.float32),
        (decay_sum.T, step_size.T, act_heads, dy_heads),
    )
    score_low = lax.psum(score_part, "tensor").astype(jnp.bfloat16)
    grad_c = jnp.dot(score_low, b_proj, preferred_element_type=jnp.float32)
    grad_b = contract_rows(score_low, c_proj)
    grad_inner = grad_heads.transpose(1, 0, 2).reshape(length, inner_local) + skip_cols * grad_y
    grad_rate = jnp.cumsum(grad_sums.T[::-1], axis=0)[::-1]
    grad_step_total = grad_steps.T + grad_rate * decay_rate
    grad_decay_local = jnp.sum(grad_rate * step_size, axis=0) * decay_rate
    grad_step_pre = grad_step_total * jax.nn.sigmoid(step_pre)
    grad_bias_local = jnp.sum(grad_step_pre, axis=0)
    grad_conv_out = jnp.concatenate([grad_inner, grad_b, grad_c], axis=1) * silu_slope(conv_out)
    grad_channels = jnp.zeros_like(channels)
    tap_grads = []
    for tap_index in range(kernel):
        offset = kernel - 1 - tap_index
        masked = grad_conv_out * conv_masks[tap_index][:, None]
        grad_channels = grad_channels + conv_local[tap_index] * shift_up(masked, offset)
        tap_grads.append(jnp.sum(masked * shift_down(channels, offset), axis=0))
    grad_taps = jnp.stack(tap_grads)
    grad_conv_sum = jnp.sum(grad_conv_out, axis=0)
    first_flag = (tensor_pos == 0).astype(jnp.float32)
    gate_low = grad_gate.astype(jnp.bfloat16)
    inner_low = grad_channels[:, :inner_local].astype(jnp.bfloat16)
    bc_low = grad_channels[:, inner_local:].astype(jnp.bfloat16)
    step_low = grad_step_pre.astype(jnp.bfloat16)
    bc_share = bc_low * first_flag.astype(jnp.bfloat16)
    grad_normed = lax.psum_scatter(
        (
            contract_cols(gate_low, back_in[0])
            + contract_cols(inner_low, back_in[1])
            + contract_cols(bc_share, back_bc)
            + contract_cols(step_low, back_step)
        ).astype(jnp.bfloat16),
        "tensor",
        scatter_dimension=0,
        tiled=True,
    ).astype(jnp.float32)
    grad_norm_gain = jnp.sum(grad_normed * resid * norm_scale, axis=0)
    pre_stat = jnp.sum(grad_normed * norm_gain * resid, axis=-1, keepdims=True)
    grad_hidden = (
        cotangent.astype(jnp.float32)
        + norm_scale * norm_gain * grad_normed
        - resid * norm_scale**3 * pre_stat / model_width
    )
    grad_in_part = jnp.stack(
        [contract_rows(normed_all, gate_low), contract_rows(normed_all, inner_low)]
    )
    grad_bc_part = contract_rows(normed_all, bc_low)
    grad_step_part = contract_rows(normed_all, step_low)
    grad_in_weight, grad_bc_weight, grad_step_weight, grad_out_weight = (
        lax.psum_scatter(grad_in_part, "dp", scatter_dimension=1, tiled=True),
        lax.psum_scatter(grad_bc_part, "dp", scatter_dimension=0, tiled=True),
        lax.psum_scatter(grad_step_part, "dp", scatter_dimension=0, tiled=True),
        lax.psum_scatter(grad_w_out, "dp", scatter_dimension=1, tiled=True),
    )
    conv_grad = jnp.zeros((kernel, inner_total + 2 * state_size), jnp.float32)
    conv_grad = lax.dynamic_update_slice(conv_grad, grad_taps[:, :inner_local], (0, inner_start))
    conv_grad = lax.dynamic_update_slice(
        conv_grad, grad_taps[:, inner_local:] * first_flag, (0, inner_total)
    )
    bias_grad = jnp.zeros((inner_total + 2 * state_size,), jnp.float32)
    bias_grad = lax.dynamic_update_slice(bias_grad, grad_conv_sum[:inner_local], (inner_start,))
    bias_grad = lax.dynamic_update_slice(
        bias_grad, grad_conv_sum[inner_local:] * first_flag, (inner_total,)
    )
    head_zeros = jnp.zeros((head_count,), jnp.float32)
    step_bias_grad = lax.dynamic_update_slice(head_zeros, grad_bias_local, (head_start,))
    decay_grad = lax.dynamic_update_slice(head_zeros, grad_decay_local, (head_start,))
    skip_grad = lax.dynamic_update_slice(head_zeros, grad_skip_local, (head_start,))
    gain_grad = lax.dynamic_update_slice(
        jnp.zeros((inner_total,), jnp.float32), grad_gain_local, (inner_start,)
    )
    summed = lax.psum(
        (conv_grad, bias_grad, step_bias_grad, decay_grad, skip_grad, gain_grad, grad_norm_gain),
        ("dp", "tensor"),
    )
    return (
        mixed,
        grad_hidden,
        summed[6],
        grad_in_weight,
        grad_bc_weight,
        grad_step_weight,
        summed[0],
        summed[1],
        summed[2],
        summed[3],
        summed[4],
        summed[5],
        grad_out_weight,
    )


def solution(mesh):
    return jax.shard_map(
        on_device,
        mesh=mesh,
        in_specs=(
            P(("dp", "tensor"), None),
            P("dp", None),
            P(),
            P(None, "dp", "tensor"),
            P("dp", None),
            P("dp", "tensor"),
            P(),
            P(),
            P(),
            P(),
            P(),
            P(),
            P("tensor", "dp"),
            P(("dp", "tensor"), None),
        ),
        out_specs=(
            P(("dp", "tensor"), None),
            P(("dp", "tensor"), None),
            P(),
            P(None, "dp", "tensor"),
            P("dp", None),
            P("dp", "tensor"),
            P(),
            P(),
            P(),
            P(),
            P(),
            P(),
            P("tensor", "dp"),
        ),
        check_vma=False,
    )
```

profile of v0, /device:TPU:25, one launch (start us, length us, event | category | flops | bytes accessed | tf_op | source)
XLA Modules:
  0.0 1510.5 jit_solution(4658288094405626091)
XLA Ops:
  14.4 86.9 %all_gather.25 = bf16[1536,256]{1,0:T(8,128)(2,1)S(1)} all-gather(bf16[24,256]{1,0:T(8,128)(2,1)S(1)} %copy-done.37), channel_id=1, replica_groups=mesh['dp'=64,'tensor'=2] {'dp'}, dimensions={0}, use_global_device_ids=true | all-gather | bytes 798720 | tf_op jit(solution)/shard_map/all_gather | solution.py:85
  102.0 96.9 %all_gather.23 = bf16[1536,24]{1,0:T(8,128)(2,1)S(1)} all-gather(bf16[24,24]{1,0:T(8,128)(2,1)S(1)} %copy-done.39), channel_id=1, replica_groups=mesh['dp'=64,'tensor'=2] {'dp'}, dimensions={0}, use_global_device_ids=true | all-gather | bytes 74880 | tf_op jit(solution)/shard_map/all_gather | solution.py:86
  206.3 4.6 fusion.49
  212.7 4.6 multiply_convert_fusion.2
  222.6 4.1 copy.69
  228.9 75.8 %while.33 = (s32[]{:T(128)}, f32[24,512,64]{1,2,0:T(8,128)}, f32[24,512]{1,0:T(8,128)S(1)}, f32[24,512]{1,0:T(8,128)}, f32[512,512]{1,0:T(8,128)}, /*index=5*/bf16[24,512,64]{2,1,0:T(8,128)(2,1)}, s32[512]{0:T(512)}) while((s32[]{:T(128)}, f32[24,512,64]{1,2,0:T(8,128)}, f32[24,512]{1,0:T(8,128)S(1)}, ...), condition=%wide.region_4.5_spmd.clone.clone.clone, body=%wide.region_3.4_spmd.clone.clone.sunk.clone | while | flops 35913728 | bytes 1330265 | solution.py:137
  304.7 3.5 copy.70
  308.2 9.6 multiply_reduce_fusion.7
  317.8 4.2 psum.70
  322.1 8.8 multiply_reduce_fusion.5
  330.9 3.8 psum.71
  334.7 7.9 fusion.61
  348.6 182.4 %while.34 = (s32[]{:T(128)}, f32[512,512]{1,0:T(8,128)}, f32[24,512,64]{1,2,0:T(8,128)}, f32[24,512]{1,0:T(8,128)S(1)}, f32[24,512]{1,0:T(8,128)}, /*index=5*/bf...) while((s32[]{:T(128)}, f32[512,512]{1,0:T(8,128)}, ...), condition=%wide.region_14.15_spmd.clone.clone.clone.clone, body=%wide.region_10.14_spmd.clone.clone.clone.sunk.clone | while | flops 73661440 | bytes 8833702 | solution.py:192
  356.6 3.5 fusion.164
  364.2 3.5 fusion.164
  371.9 3.5 fusion.164
  379.5 3.5 fusion.164
  387.1 3.5 fusion.164
  394.7 3.5 fusion.164
  410.0 3.5 fusion.164
  417.6 3.5 fusion.164
  425.2 3.5 fusion.164
  440.4 3.5 fusion.164
  455.6 3.5 fusion.164
  470.9 3.5 fusion.164
  478.5 3.5 fusion.164
  486.1 3.5 fusion.164
  501.3 3.5 fusion.164
  508.9 3.5 fusion.164
  516.5 3.5 fusion.164
  524.1 3.5 fusion.164
  531.7 25.6 %all-reduce.15 = bf16[512,512]{1,0:T(8,128)(2,1)} all-reduce(f32[512,512]{1,0:T(8,128)} %get-tuple-element.122), channel_id=1, replica_groups=mesh['dp'=64,'tensor'=2] {'tensor'}, use_global_device_ids=true, to_apply=%region_15.16 | all-reduce | flops 262144 | bytes 1572864 | tf_op jit(solution)/shard_map/psum | solution.py:197
  560.7 3.6 copy.74
  564.3 4.3 multiply_add_fusion.1
  570.7 8.3 multiply_reduce_fusion.4
  581.2 5.2 fusion.48
  586.4 4.6 fusion.59
  593.9 7.2 convolution_convert_fusion
  607.4 19.7 %reduce-scatter.11.cloned.1.call-done = bf16[256,1536]{1,0:T(8,128)(2,1)} async-done(((bf16[512,1536]{1,0:T(8,128)(2,1)}), bf16[256,1536]{1,0:T(8,128)(2,1)}) %reduce-scatter.11.cloned.1.call-update) | async-done | bytes 786448 | tf_op jit(solution)/shard_map/reduce_scatter | solution.py:222
  629.4 8.8 fusion.118
  638.3 4.4 convolution_bitcast_fusion.2
  645.4 6.8 pad_maximum_fusion
  652.3 6.9 reduce-scatter.9.cloned.1.call-done
  662.4 142.7 %reduce-scatter.19.cloned.1.call-done = f32[24,24]{1,0:T(8,128)} async-done(((f32[1536,24]{1,0:T(8,128)}), f32[24,24]{1,0:T(8,128)}) %reduce-scatter.19.cloned.1.call-update) | async-done | bytes 2320
  805.0 146.5 %reduce-scatter.15.cloned.1.call-done = f32[24,256]{1,0:T(8,128)} async-done(((f32[1536,256]{1,0:T(8,128)}), f32[24,256]{1,0:T(8,128)}) %reduce-scatter.15.cloned.1.call-update) | async-done | bytes 24592 | tf_op jit(solution)/shard_map/reduce_scatter | solution.py:247
  951.5 149.2 %all-reduce.14.cloned.1.call-done = (f32[1536]{0:T(1024)}, f32[4,3328]{1,0:T(4,128)}, f32[3328]{0:T(1024)}, f32[48]{0:T(128)}, f32[48]{0:T(128)}, /*index=5*/f32[48]{0:T(128)}, f32[3072]{0:T(1024)}) async-done(((f32[1536]{0:T(1024)}, f32[4,3328]{1,0:T(4,128)}, f32[3328]{0:T(1024)}, f32[48]{0:T(128)}, f32[48]{0:T(128)}, /*index=5*/f32[48]{0:T(128)}, f32[3072]{0:T(1024)}), (f32[1536]{0:T(1024)}, ...) | async-done | bytes 85584 | tf_op jit(solution)/shard_map/psum | solution.py:268
  1100.7 176.5 %reduce-scatter.17.cloned.1.call-done = f32[1536,24]{0,1:T(8,128)} async-done(((f32[1536,1536]{0,1:T(8,128)}), f32[1536,24]{0,1:T(8,128)}) %reduce-scatter.17.cloned.1.call-update) | async-done | bytes 147472 | tf_op jit(solution)/shard_map/reduce_scatter | solution.py:249
  1277.2 217.9 %reduce-scatter.13.cloned.1.call-done = f32[2,24,1536]{2,1,0:T(8,128)} async-done(((f32[2,1536,1536]{2,1,0:T(8,128)}), f32[2,24,1536]{2,1,0:T(8,128)}) %reduce-scatter.13.cloned.1.call-update) | async-done | bytes 294928 | tf_op jit(solution)/shard_map/reduce_scatter | solution.py:246
  (441 shorter events, 259.2 us)
Async XLA Ops:
  7.2 7.1 copy-start.34
  7.2 192.1 %slice-start = ((f32[4,3328]{1,0:T(4,128)}), f32[4,256]{1,0:T(4,128)S(1)}, s32[]{:S(2)}) async-start(f32[4,3328]{1,0:T(4,128)} %param.24), calls=%async_computation.17 | async-start | bytes 8192 | tf_op jit(solution)/shard_map/slice | solution.py:102
  7.2 7.1 copy-start.41
  7.2 192.2 %slice-start.1 = ((f32[3328]{0:T(1024)}), f32[256]{0:T(256)S(1)}, s32[]{:S(2)}) async-start(f32[3328]{0:T(1024)} %param.25), calls=%async_computation.18 | async-start | bytes 2048 | tf_op jit(solution)/shard_map/slice | solution.py:107
  7.2 7.2 copy-start.37
  7.2 94.0 %copy-start.45 = (s32[1,512]{1,0:T(1,128)S(1)}, s32[1,512]{1,0:T(1,128)}, u32[]{:S(2)}) copy-start(s32[1,512]{1,0:T(1,128)} %param.19) | copy-start | bytes 6148
  7.2 94.8 %copy-start.39 = (bf16[24,24]{1,0:T(8,128)(2,1)S(1)}, bf16[24,24]{1,0:T(8,128)(2,1)}, u32[]{:S(2)}) copy-start(bf16[24,24]{1,0:T(8,128)(2,1)} %param.23) | copy-start | bytes 3460
  7.3 191.7 %copy-start.52 = (f32[48]{0:T(128)S(1)}, f32[48]{0:T(128)}, u32[]{:S(2)}) copy-start(f32[48]{0:T(128)} %param.26) | copy-start | bytes 580
  7.3 191.8 %copy-start.50 = (f32[48]{0:T(128)S(1)}, f32[48]{0:T(128)}, u32[]{:S(2)}) copy-start(f32[48]{0:T(128)} %param.27) | copy-start | bytes 580
  7.3 191.8 %copy-start.53 = (f32[48]{0:T(128)S(1)}, f32[48]{0:T(128)}, u32[]{:S(2)}) copy-start(f32[48]{0:T(128)} %param.28) | copy-start | bytes 580
  7.3 192.8 %copy-start.40 = (f32[3072]{0:T(1024)S(1)}, f32[3072]{0:T(1024)}, u32[]{:S(2)}) copy-start(f32[3072]{0:T(1024)} %param.29) | copy-start | bytes 36868
  7.3 192.8 %all-gather.5.cloned.1.call-start = ((), (), s32[]{:S(2)}) async-start(), calls=%async_computation.6 | async-start | bytes 2359296 | tf_op jit(solution)/shard_map/all_gather | solution.py:92
  12.1 194.2 %all-gather.7.cloned.1.call-start = ((), (), s32[]{:S(2)}) async-start(), calls=%async_computation.7 | async-start | bytes 9584640 | tf_op jit(solution)/shard_map/all_gather | solution.py:84
  12.9 309.2 %all-gather.11.cloned.1.call-start = ((), (), s32[]{:S(2)}) async-start(), calls=%async_computation.10 | async-start | bytes 2359296 | tf_op jit(solution)/shard_map/all_gather | solution.py:156
  13.6 308.5 %all-gather.9.cloned.1.call-start = ((), (), s32[]{:S(2)}) async-start(), calls=%async_computation.8 | async-start | bytes 4792320 | tf_op jit(solution)/shard_map/all_gather | solution.py:87
  14.2 612.9 %reduce-scatter.11.cloned.1.call-start = ((), (), s32[]{:S(2)}) async-start(), calls=%async_computation.11 | async-start | bytes 2359296 | tf_op jit(solution)/shard_map/reduce_scatter | solution.py:222
  101.2 109.7 %copy-start.7 = (bf16[1536,256]{1,0:T(8,128)(2,1)}, bf16[1536,256]{1,0:T(8,128)(2,1)S(1)}, u32[]{:S(2)}) copy-start(bf16[1536,256]{1,0:T(8,128)(2,1)S(1)} %all_gather.25) | copy-start | bytes 2359300
  198.9 5.3 copy-start.11
  199.1 5.1 copy-start.43
  200.1 6.2 copy-start.1
  206.3 4.7 copy-start.9
  217.3 90.9 %copy-start.3 = (bf16[512,1792]{1,0:T(8,128)(2,1)}, bf16[512,1792]{1,0:T(8,128)(2,1)S(1)}, u32[]{:S(2)}) copy-start(bf16[512,1792]{1,0:T(8,128)(2,1)S(1)} %get-tuple-element.388) | copy-start | bytes 5505028
  322.1 12.6 copy-start.27
  344.0 4.6 copy-start.22
  344.0 4.6 copy-start.46
  570.7 8.3 copy-start.5
  570.7 8.4 copy-start.10
  581.1 9.9 copy-start.15
  581.1 5.2 copy-start.16
  593.9 7.4 copy-start.2
  593.9 65.2 %reduce-scatter.9.cloned.1.call-start = ((), (), s32[]{:S(2)}) async-start(), calls=%async_computation.9 | async-start | bytes 2359296 | tf_op jit(solution)/shard_map/reduce_scatter | solution.py:149
  601.2 203.8 %reduce-scatter.19.cloned.1.call-start = ((), (), s32[]{:S(2)}) async-start(), calls=%async_computation.15 | async-start | bytes 798720
  602.8 24.3 %copy-start.6 = (bf16[256,1536]{1,0:T(8,128)(2,1)S(1)}, bf16[256,1536]{1,0:T(8,128)(2,1)}, u32[]{:S(2)}) copy-start(bf16[256,1536]{1,0:T(8,128)(2,1)} %param.18) | copy-start | bytes 2359300
  602.8 24.3 %copy-start.20 = (f32[1536]{0:T(1024)S(1)}, f32[1536]{0:T(1024)}, u32[]{:S(2)}) copy-start(f32[1536]{0:T(1024)} %param.20) | copy-start | bytes 18436
  602.8 24.3 %copy-start.36 = (f32[256]{0:T(256)S(1)}, f32[256]{0:T(256)}, u32[]{:S(2)}) copy-start(f32[256]{0:T(256)} %copy-done.35) | copy-start | bytes 3076
  602.8 348.7 %reduce-scatter.15.cloned.1.call-start = ((), (), s32[]{:S(2)}) async-start(), calls=%async_computation.13 | async-start | bytes 1597440 | tf_op jit(solution)/shard_map/reduce_scatter | solution.py:247
  605.7 495.0 %all-reduce.14.cloned.1.call-start = ((), (), s32[]{:S(2)}) async-start(), calls=%async_computation.16 | async-start | bytes 183296 | tf_op jit(solution)/shard_map/psum | solution.py:268
  606.1 23.2 %copy-start.48 = (f32[48]{0:T(128)}, f32[48]{0:T(128)S(1)}, u32[]{:S(2)}) copy-start(f32[48]{0:T(128)S(1)} %dynamic_update_slice.42) | copy-start | bytes 580
  606.4 22.9 %copy-start.49 = (f32[48]{0:T(128)}, f32[48]{0:T(128)S(1)}, u32[]{:S(2)}) copy-start(f32[48]{0:T(128)S(1)} %dynamic_update_slice.44) | copy-start | bytes 580
  606.8 22.5 %copy-start.26 = (f32[3072]{0:T(1024)}, f32[3072]{0:T(1024)S(1)}, u32[]{:S(2)}) copy-start(f32[3072]{0:T(1024)S(1)} %dynamic_update_slice.45) | copy-start | bytes 36868
  606.9 22.5 %copy-start.19 = (f32[4,3328]{1,0:T(4,128)}, f32[4,3328]{1,0:T(4,128)S(1)}, u32[]{:S(2)}) copy-start(f32[4,3328]{1,0:T(4,128)S(1)} %fusion.110) | copy-start | bytes 159748
  607.1 22.2 %copy-start.47 = (f32[48]{0:T(128)}, f32[48]{0:T(128)S(1)}, u32[]{:S(2)}) copy-start(f32[48]{0:T(128)S(1)} %multiply_dynamic-update-slice_fusion) | copy-start | bytes 580
  607.4 22.0 %copy-start.21 = (f32[3328]{0:T(1024)}, f32[3328]{0:T(1024)S(1)}, u32[]{:S(2)}) copy-start(f32[3328]{0:T(1024)S(1)} %fusion.117) | copy-start | bytes 39940
  629.4 647.8 %reduce-scatter.17.cloned.1.call-start = ((), (), s32[]{:S(2)}) async-start(), calls=%async_computation.14 | async-start | bytes 9584640 | tf_op jit(solution)/shard_map/reduce_scatter | solution.py:249
  638.3 856.8 %reduce-scatter.13.cloned.1.call-start = ((), (), s32[]{:S(2)}) async-start(), calls=%async_computation.12 | async-start | bytes 19169280 | tf_op jit(solution)/shard_map/reduce_scatter | solution.py:246
  652.2 6.9 copy-start.13
  652.2 6.9 copy-start.14
  652.2 6.9 copy-start.42
  (42 other events, 126.5 us)
Sparse Core Ops, SparseCore 0:
  12.3 32.8 all-gather.4
  48.3 86.5 all-gather.6
  136.6 27.8 all-gather.10
  167.4 73.8 all-gather.8
  594.0 33.0 reduce-scatter.10
  629.4 29.6 reduce-scatter.8
  664.7 140.2 reduce-scatter.18
  810.7 140.7 reduce-scatter.14
  959.8 140.8 all-reduce.13
  1106.9 170.2 reduce-scatter.16
  1284.9 210.1 reduce-scatter.12
where the time goes:
time: 1530 us; the launch traced here: 1510 us
  waiting for transfers between devices  861 us (56%)
  matrix products  262 us (17%)
  blocking collectives  217 us (14%)
  local copies, waits for them, and re-layouts  104 us (7%)
  other arithmetic  50.7 us (3%)
    reduce_scatter x1, waiting for transfers between devices, on_device(): lax.psum_scatter(grad_in_part, 'dp', scatter_dimension=1, tiled=True)  218 us
    reduce_scatter x1, waiting for transfers between devices, on_device(): lax.psum_scatter(grad_w_out, 'dp', scatter_dimension=1, tiled=True)  177 us
    psum x1, waiting for transfers between devices, on_device(): lax.psum((conv_grad, bias_grad, step_bias_grad, decay_grad, skip_grad, ga...  149 us
    reduce_scatter x1, waiting for transfers between devices, on_device(): lax.psum_scatter(grad_bc_part, 'dp', scatter_dimension=0, tiled=True)  146 us
    unnamed x12, waiting for transfers between devices  145 us
    dot_general x30, matrix products, contract_cols(): lax.dot_general(left, right, (((1,), (1,)), ((), ())), preferred_element_...  106 us
    all_gather x1, blocking collectives, on_device(): lax.all_gather(step_weight, 'dp', axis=0, tiled=True)  96.9 us
    all_gather x1, blocking collectives, on_device(): lax.all_gather(bc_weight, 'dp', axis=0, tiled=True)  86.9 us
  transfers between devices with their start and end apart: 11, of which 7 were waited for; matrix products, arithmetic and copies ran while one was open for 11% of the time, Pallas kernels for 0%

commit v1 on v0

v1 whole, which is shorter than its diff:
```python
import jax
import jax.numpy as jnp
from jax import lax
from jax.experimental import pallas as pl
from jax.experimental.pallas import tpu as pltpu
from jax.sharding import PartitionSpec as P

EPS = 1e-05
LOG2E = 1.4426950408889634
BF = jnp.bfloat16
F32 = jnp.float32
LEN = 512
TILE = 128
BLOCK = 256
VMEM_BYTES = 50 * 1024 * 1024

SWAP = [(0, 1), (1, 0)]


def dp_index(x, z, y, c):
    return ((x * 2 + z) * 4 + y) * 2 + c


def dp_pairs(move):
    return [
        (dp_index(x, z, y, c), dp_index(*move(x, z, y, c)))
        for x in range(4)
        for z in range(2)
        for y in range(4)
        for c in range(2)
    ]


CORE = dp_pairs(lambda x, z, y, c: (x, z, y, 1 - c))
ZHI = dp_pairs(lambda x, z, y, c: (x, 1 - z, y, c))
XS = {k: dp_pairs(lambda x, z, y, c, k=k: ((x + k) % 4, z, y, c)) for k in (1, 2, 3)}
YS = {k: dp_pairs(lambda x, z, y, c, k=k: (x, z, (y + k) % 4, c)) for k in (1, 2, 3)}
PLANES = [[2 * i + c for i in range(32)] for c in range(2)]


def send(values, pairs):
    return lax.ppermute(values, "dp", pairs)


def swap_tensor(values):
    return lax.ppermute(values, "tensor", SWAP)


def place(pieces, spots, axis, count):
    shape = list(pieces[0].shape)
    shape.insert(axis, count)
    whole = jnp.zeros(tuple(shape), pieces[0].dtype)
    for piece, spot in zip(pieces, spots):
        start = [0] * len(shape)
        start[axis] = spot
        whole = lax.dynamic_update_slice(whole, jnp.expand_dims(piece, axis), tuple(start))
    return whole


def ring_gather(values, perms, here, axis):
    pieces = [values] + [send(values, perms[k]) for k in (1, 3, 2)]
    return place(pieces, [here, (here + 3) % 4, (here + 1) % 4, (here + 2) % 4], axis, 4)


def gather_rows(own, spot):
    x, z, y, c = spot
    half = own.shape[1] // 2
    mine = lax.dynamic_slice_in_dim(own, c * half, half, 1)
    got = send(lax.dynamic_slice_in_dim(own, (1 - c) * half, half, 1), CORE)
    rows = jnp.concatenate([jnp.where(c == 0, mine, got), jnp.where(c == 0, got, mine)], 0)
    other = send(rows, ZHI)
    both = jnp.stack([jnp.where(z == 0, rows, other), jnp.where(z == 0, other, rows)], 0)
    part_a = ring_gather(both[..., : half // 2], YS, y, 1)
    part_b = ring_gather(both[..., half // 2 :], XS, x, 0)
    part_a = ring_gather(part_a, XS, x, 0)
    part_b = ring_gather(part_b, YS, y, 2)
    peer_a, peer_b = send(part_a, CORE), send(part_b, CORE)
    return tuple(v.reshape(1536, half // 2) for v in (part_a, part_b, peer_a, peer_b))


def reduce_rows(own, peer, c):
    got = send(peer.astype(BF), CORE)
    pair = (own + got.astype(F32)).astype(BF).reshape(32, 48, own.shape[1])
    spread = lax.all_to_all(pair, "dp", 0, 0, tiled=True, axis_index_groups=PLANES)
    total = jnp.sum(spread.astype(F32), axis=0)
    mine = lax.dynamic_slice_in_dim(total, c * 24, 24, 0)
    other = send(lax.dynamic_slice_in_dim(total, (1 - c) * 24, 24, 0), CORE)
    return mine, other


def reduce_small(values):
    values = values + send(values, CORE)
    values = values + send(values, ZHI)
    for perms in (YS, XS):
        got = [send(values, perms[k]) for k in (1, 2, 3)]
        values = (values + got[1]) + (got[0] + got[2])
    return values


def dot(left, right):
    return jnp.dot(left, right, preferred_element_type=F32)


def dot_rows(left, right):
    return lax.dot_general(left, right, (((0,), (0,)), ((), ())), preferred_element_type=F32)


def dot_cols(left, right):
    return lax.dot_general(left, right, (((1,), (1,)), ((), ())), preferred_element_type=F32)


def silu_slope(values):
    sig = jax.nn.sigmoid(values)
    return sig * (1.0 + values * (1.0 - sig))


def down(values, offset):
    return values if offset == 0 else pltpu.roll(values, offset, 0)


def up(values, offset):
    return values if offset == 0 else pltpu.roll(values, values.shape[0] - offset, 0)


def conv_of(pre, taps, bias, masks):
    out = bias + taps[3:4] * pre
    for offset in (1, 2, 3):
        out = out + taps[3 - offset : 4 - offset] * (down(pre, offset) * masks[:, offset : offset + 1])
    return out


def lane_halves(values):
    low = lax.broadcasted_iota(jnp.int32, (1, TILE), 1) < 64
    zero = jnp.zeros_like(values)
    return jnp.where(low, values, zero), jnp.where(low, zero, values)


def params(semantics="arbitrary"):
    return pltpu.CompilerParams(dimension_semantics=(semantics,), vmem_limit_bytes=VMEM_BYTES)


def mix_kernel(normed, own_a, own_b, peer_a, peer_b, taps, bias, masks, scores, cols, rows, pre, act, mixed):
    step = pl.program_id(0)
    for test, weight in (
        (step < 2, own_a),
        (step == 2, own_b),
        ((step == 3) | (step == 4), peer_a),
        (step == 5, peer_b),
    ):

        @pl.when(test)
        def _(weight=weight):
            pre[...] = dot(normed[...], weight[...])

    conv_out = conv_of(pre[...], taps[...], bias[...], masks[...])
    act[...] = (conv_out * jax.nn.sigmoid(conv_out)).astype(BF)
    for pair in range(2):
        lanes = slice(pair * TILE, (pair + 1) * TILE)
        halves = lane_halves(act[:, lanes])
        for tile in range(4):
            here = slice(tile * TILE, (tile + 1) * TILE)
            weights, values = [], []
            for side in range(2):
                head = 2 * pair + side
                sums = cols[0, here, head : head + 1]
                if tile:
                    decay = jnp.exp2(sums - rows[0, 4 + head : 5 + head, : tile * TILE])
                    weights.append((scores[here, : tile * TILE] * decay).astype(BF))
                    values.append(halves[side][: tile * TILE])
                decay = jnp.exp2(
                    jnp.minimum(sums - rows[0, 4 + head : 5 + head, here], rows[0, 8 + head : 9 + head, here])
                )
                weights.append((scores[here, here] * decay).astype(BF))
                values.append(halves[side][here])
            mixed[here, lanes] = dot(jnp.concatenate(weights, 1), jnp.concatenate(values, 0))


def mix_forward(normed, weights, taps, bias, masks, scores, cols, rows):
    full = lambda *shape: pl.BlockSpec(shape, lambda i: (0,) * len(shape))
    block = lambda count: pl.BlockSpec((count, BLOCK), lambda i: (0, i))
    return pl.pallas_call(
        mix_kernel,
        grid=(6,),
        in_specs=[
            full(LEN, 1536),
            pl.BlockSpec((1536, BLOCK), lambda i: (0, jnp.minimum(i, 1))),
            pl.BlockSpec((1536, BLOCK), lambda i: (0, 0)),
            pl.BlockSpec((1536, BLOCK), lambda i: (0, jnp.clip(i - 3, 0, 1))),
            pl.BlockSpec((1536, BLOCK), lambda i: (0, 0)),
            block(4),
            block(1),
            full(LEN, 4),
            full(LEN, LEN),
            pl.BlockSpec((1, LEN, 16), lambda i: (i, 0, 0)),
            pl.BlockSpec((1, 16, LEN), lambda i: (i, 0, 0)),
        ],
        out_specs=[block(LEN)] * 3,
        out_shape=[
            jax.ShapeDtypeStruct((LEN, 1536), F32),
            jax.ShapeDtypeStruct((LEN, 1536), BF),
            jax.ShapeDtypeStruct((LEN, 1536), F32),
        ],
        compiler_params=params(),
        cost_estimate=pl.CostEstimate(flops=4_000_000_000, bytes_accessed=16_000_000, transcendentals=5_000_000),
        name="mix_forward",
    )(normed, *weights, taps, bias, masks, scores, cols, rows)


def gate_kernel(normed, cot, gate_own, gate_peer, out_own, out_peer, act, mixed, skip, gain, gate_pre, grad_gn, stats, squares, dots):
    step = pl.program_id(0)
    for test, gate_w, out_w in ((step < 3, gate_own, out_own), (step >= 3, gate_peer, out_peer)):

        @pl.when(test)
        def _(gate_w=gate_w, out_w=out_w):
            gate_pre[...] = dot(normed[...], gate_w[...])
            grad_gn[...] = dot(cot[...], out_w[...])

    @pl.when(step == 0)
    def _():
        squares[...] = jnp.zeros_like(squares)
        dots[...] = jnp.zeros_like(dots)

    pre = gate_pre[...]
    mixer_y = mixed[...] + skip[...] * act[...].astype(F32)
    gated = mixer_y * (pre * jax.nn.sigmoid(pre))
    square = gated * gated
    product = grad_gn[...] * gain[...] * gated
    squares[...] += square[:, :TILE] + square[:, TILE:]
    dots[...] += product[:, :TILE] + product[:, TILE:]

    @pl.when(step == 5)
    def _():
        stats[0:1, :] = jnp.sum(squares[...].T, axis=0, keepdims=True)
        stats[1:2, :] = jnp.sum(dots[...].T, axis=0, keepdims=True)
        stats[2:8, :] = jnp.zeros((6, LEN), F32)


def gate_forward(normed, cot, gate_w, out_w, act, mixed, skip, gain):
    full = lambda *shape: pl.BlockSpec(shape, lambda i: (0,) * len(shape))
    block = lambda count: pl.BlockSpec((count, BLOCK), lambda i: (0, i))
    early = pl.BlockSpec((1536, BLOCK), lambda i: (0, jnp.minimum(i, 2)))
    late = pl.BlockSpec((1536, BLOCK), lambda i: (0, jnp.maximum(i - 3, 0)))
    return pl.pallas_call(
        gate_kernel,
        grid=(6,),
        in_specs=[full(LEN, 1536), full(LEN, 1536), early, late, early, late, block(LEN), block(LEN), block(1), block(1)],
        out_specs=[block(LEN), block(LEN), full(8, LEN)],
        out_shape=[
            jax.ShapeDtypeStruct((LEN, 1536), F32),
            jax.ShapeDtypeStruct((LEN, 1536), F32),
            jax.ShapeDtypeStruct((8, LEN), F32),
        ],
        scratch_shapes=[pltpu.VMEM((LEN, TILE), F32)] * 2,
        compiler_params=params(),
        cost_estimate=pl.CostEstimate(flops=4_900_000_000, bytes_accessed=24_000_000, transcendentals=800_000),
        name="gate_forward",
    )(normed, cot, *gate_w, *out_w, act, mixed, skip, gain)


def slope_kernel(stats, gate_pre, grad_gn, act, mixed, skip, gain, gate_low, gnormed, grad_y, gain_grad, scale, dots):
    @pl.when(pl.program_id(0) == 0)
    def _():
        inv = lax.rsqrt(stats[0:1, :] * (1.0 / 3072.0) + EPS)
        scale[...] = jnp.broadcast_to(inv, (TILE, LEN)).T
        dots[...] = jnp.broadcast_to(inv * inv * inv * stats[1:2, :] * (1.0 / 3072.0), (TILE, LEN)).T

    for part in range(2):
        lanes = slice(part * TILE, (part + 1) * TILE)
        q = scale[...]
        pre = gate_pre[:, lanes]
        sig = jax.nn.sigmoid(pre)
        gate_act = pre * sig
        mixer_y = mixed[:, lanes] + skip[:, lanes] * act[:, lanes].astype(F32)
        gated = mixer_y * gate_act
        scaled = gated * q
        gnormed[:, lanes] = (scaled * gain[:, lanes]).astype(BF)
        upper = grad_gn[:, lanes]
        gain_grad[:, lanes] = jnp.sum(upper * scaled, axis=0, keepdims=True)
        grad_gated = q * gain[:, lanes] * upper - gated * dots[...]
        grad_y[:, lanes] = grad_gated * gate_act
        gate_low[:, lanes] = (grad_gated * mixer_y * (sig * (1.0 + pre * (1.0 - sig)))).astype(BF)


def gate_backward(stats, gate_pre, grad_gn, act, mixed, skip, gain):
    full = lambda *shape: pl.BlockSpec(shape, lambda i: (0,) * len(shape))
    block = lambda count: pl.BlockSpec((count, BLOCK), lambda i: (0, i))
    return pl.pallas_call(
        slope_kernel,
        grid=(6,),
        in_specs=[full(8, LEN), block(LEN), block(LEN), block(LEN), block(LEN), block(1), block(1)],
        out_specs=[block(LEN), block(LEN), block(LEN), block(1)],
        out_shape=[
            jax.ShapeDtypeStruct((LEN, 1536), BF),
            jax.ShapeDtypeStruct((LEN, 1536), BF),
            jax.ShapeDtypeStruct((LEN, 1536), F32),
            jax.ShapeDtypeStruct((1, 1536), F32),
        ],
        scratch_shapes=[pltpu.VMEM((LEN, TILE), F32)] * 2,
        compiler_params=params(),
        cost_estimate=pl.CostEstimate(flops=20_000_000, bytes_accessed=18_000_000, transcendentals=800_000),
        name="gate_backward",
    )(stats, gate_pre, grad_gn, act, mixed, skip, gain)


def back_kernel(grad_y, act, mixed, pre, scores, taps, bias, masks, cols, rows, skip, inner_low, sums, flows, grad_scores, grad_act):
    step = pl.program_id(0)

    @pl.when(step == 0)
    def _():
        grad_scores[...] = jnp.zeros_like(grad_scores)

    pairs = []
    for pair in range(2):
        lanes = slice(pair * TILE, (pair + 1) * TILE)
        low = grad_y[:, lanes].astype(BF)
        pairs.append((lane_halves(act[:, lanes]), low, lane_halves(low)))
    for tile in range(4):
        here = slice(tile * TILE, (tile + 1) * TILE)
        after = slice((tile + 1) * TILE, LEN)
        add_diag, add_rest = 0.0, 0.0
        for pair in range(2):
            act_halves, low, low_halves = pairs[pair]
            weights, values = [], []
            for side in range(2):
                head = 2 * pair + side
                back = cols[0, here, 4 + head : 5 + head]
                most = cols[0, here, 8 + head : 9 + head]
                mine = act_halves[side][here]
                decay = jnp.exp2(jnp.minimum(rows[0, head : head + 1, here] - back, most))
                grad_w = dot_cols(mine, low[here])
                add_diag = add_diag + grad_w * decay
                weights.append((scores[here, here] * decay).astype(BF))
                values.append(low_halves[side][here])
                if tile < 3:
                    decay = jnp.exp2(rows[0, head : head + 1, after] - back)
                    grad_w = dot_cols(mine, low[after])
                    add_rest = add_rest + grad_w * decay
                    weights.append((scores[here, after] * decay).astype(BF))
                    values.append(low_halves[side][after])
            lanes = slice(pair * TILE, (pair + 1) * TILE)
            grad_act[here, lanes] = dot(jnp.concatenate(weights, 1), jnp.concatenate(values, 0))
        grad_scores[here, here] += add_diag
        if tile < 3:
            grad_scores[here, after] += add_rest

    low_lane = lax.broadcasted_iota(jnp.int32, (1, TILE), 1) < 64
    for pair in range(2):
        lanes = slice(pair * TILE, (pair + 1) * TILE)
        values = act[:, lanes].astype(F32)
        grad = grad_y[:, lanes]
        row_flow = grad.astype(BF).astype(F32) * mixed[:, lanes]
        col_flow = values * grad_act[:, lanes]
        for side, mask in ((0, low_lane), (1, ~low_lane)):
            head = 2 * pair + side
            flows[0, :, head : head + 1] = jnp.sum(jnp.where(mask, row_flow, 0.0), axis=1, keepdims=True)
            flows[0, :, 4 + head : 5 + head] = jnp.sum(jnp.where(mask, col_flow, 0.0), axis=1, keepdims=True)
        taps_l, masks_v = taps[:, lanes], masks[...]
        pre_l = pre[:, lanes]
        conv_out = conv_of(pre_l, taps_l, bias[:, lanes], masks_v)
        grad_conv = (grad_act[:, lanes] + skip[:, lanes] * grad) * silu_slope(conv_out)
        grad_pre = taps_l[3:4] * grad_conv
        sums[3:4, lanes] = jnp.sum(grad_conv * pre_l, axis=0, keepdims=True)
        for offset in (1, 2, 3):
            masked = grad_conv * masks_v[:, offset : offset + 1]
            tap = 3 - offset
            sums[tap : tap + 1, lanes] = jnp.sum(masked * down(pre_l, offset), axis=0, keepdims=True)
            grad_pre = grad_pre + taps_l[tap : tap + 1] * up(masked, offset)
        sums[4:5, lanes] = jnp.sum(grad_conv, axis=0, keepdims=True)
        sums[5:6, lanes] = jnp.sum(grad * values, axis=0, keepdims=True)
        sums[6:8, lanes] = jnp.zeros((2, TILE), F32)
        inner_low[:, lanes] = grad_pre.astype(BF)


def mix_backward(grad_y, act, mixed, pre, scores_t, taps, bias, masks, cols, rows, skip):
    full = lambda *shape: pl.BlockSpec(shape, lambda i: (0,) * len(shape))
    block = lambda count: pl.BlockSpec((count, BLOCK), lambda i: (0, i))
    return pl.pallas_call(
        back_kernel,
        grid=(6,),
        in_specs=[
            block(LEN),
            block(LEN),
            block(LEN),
            block(LEN),
            full(LEN, LEN),
            block(4),
            block(1),
            full(LEN, 4),
            pl.BlockSpec((1, LEN, 16), lambda i: (i, 0, 0)),
            pl.BlockSpec((1, 16, LEN), lambda i: (i, 0, 0)),
            block(1),
        ],
        out_specs=[
            block(LEN),
            block(8),
            pl.BlockSpec((1, LEN, 8), lambda i: (i, 0, 0)),
            full(LEN, LEN),
        ],
        out_shape=[
            jax.ShapeDtypeStruct((LEN, 1536), BF),
            jax.ShapeDtypeStruct((8, 1536), F32),
            jax.ShapeDtypeStruct((6, LEN, 8), F32),
            jax.ShapeDtypeStruct((LEN, LEN), F32),
        ],
        scratch_shapes=[pltpu.VMEM((LEN, BLOCK), F32)],
        compiler_params=params(),
        cost_estimate=pl.CostEstimate(flops=4_000_000_000, bytes_accessed=14_000_000, transcendentals=5_000_000),
        name="mix_backward",
    )(grad_y, act, mixed, pre, scores_t, taps, bias, masks, cols, rows, skip)


def on_device(
    hidden,
    segments,
    norm_gain,
    in_weight,
    bc_weight,
    step_weight,
    conv_weight,
    conv_bias,
    step_bias,
    decay_log,
    skip_gain,
    gate_gain,
    out_weight,
    cotangent,
):
    t = lax.axis_index("tensor")
    d = lax.axis_index("dp")
    spot = (d // 16, (d // 8) % 2, (d // 2) % 4, d % 2)
    c = spot[3]

    def tokens(mine):
        other = swap_tensor(mine)
        return jnp.concatenate([jnp.where(t == 0, mine, other), jnp.where(t == 0, other, mine)], 0)

    def own_first(values, size):
        base = 2 * t * size
        return jnp.concatenate(
            [
                lax.dynamic_slice_in_dim(values, base + c * size, size, values.ndim - 1),
                lax.dynamic_slice_in_dim(values, base + (1 - c) * size, size, values.ndim - 1),
            ],
            values.ndim - 1,
        )

    def natural(values, size):
        return jnp.where(c == 0, values, jnp.concatenate([values[..., size:], values[..., :size]], -1))

    hidden_all = tokens(hidden)
    step_pad = jnp.zeros((24, 116), BF)
    first = jnp.concatenate(
        [
            piece
            for j in range(2)
            for piece in (
                in_weight[1][:, j * 768 : (j + 1) * 768],
                bc_weight[:, j * 128 : (j + 1) * 128],
                step_weight[:, j * 12 : (j + 1) * 12],
                step_pad,
            )
        ],
        1,
    )
    out_rows = out_weight.T
    second = jnp.concatenate(
        [
            piece
            for j in range(2)
            for piece in (in_weight[0][:, j * 768 : (j + 1) * 768], out_rows[:, j * 768 : (j + 1) * 768])
        ],
        1,
    )
    inner_w = gather_rows(first, spot)
    own_a, own_b, peer_a, peer_b = inner_w
    gate_own, out_own, gate_peer, out_peer = gather_rows(second, spot)
    cot_all = tokens(cotangent)

    resid = hidden_all.astype(F32)
    norm_scale = lax.rsqrt(jnp.mean(resid * resid, axis=-1, keepdims=True) + EPS)
    normed = (resid * norm_scale * norm_gain).astype(BF)

    taps = own_first(conv_weight[:, :3072], 768)
    bias = own_first(conv_bias[None, :3072], 768)
    gain = own_first(gate_gain[None, :], 768)
    skip = jnp.repeat(own_first(skip_gain, 12), 64)[None, :]
    rate = -jnp.exp(own_first(decay_log, 12))
    step_off = own_first(step_bias, 12)

    seg = segments[0]
    masks = jnp.stack(
        [(jnp.pad(seg, (o, 0), constant_values=-1)[:LEN] == seg).astype(F32) for o in range(4)], 1
    )
    where_at = jnp.arange(LEN)
    visible = ((where_at[:, None] >= where_at[None, :]) & (seg[:, None] == seg[None, :])).astype(F32)

    tail_own = dot(normed, own_b[:, 256:])
    tail_peer = dot(normed, peer_b[:, 256:])
    bc_pre = jnp.concatenate(
        [
            jnp.where(c == 0, tail_own, tail_peer)[:, :128],
            jnp.where(c == 0, tail_peer, tail_own)[:, :128],
        ],
        1,
    )
    bc_taps, bc_bias = conv_weight[:, 3072:], conv_bias[3072:]

    def shifted(values, offset):
        return values if offset == 0 else jnp.pad(values, ((offset, 0), (0, 0)))[:LEN]

    bc_conv = bc_bias
    for o in range(4):
        bc_conv = bc_conv + bc_taps[3 - o] * shifted(bc_pre, o) * masks[:, o : o + 1]
    bc_act = jax.nn.silu(bc_conv).astype(BF)
    b_proj, c_proj = bc_act[:, :128], bc_act[:, 128:]
    scores = dot_cols(c_proj, b_proj) * visible
    scores_t = dot_cols(b_proj, c_proj) * visible.T

    step_pre = jnp.concatenate([tail_own[:, 128:140], tail_peer[:, 128:140]], 1) + step_off
    step_size = jax.nn.softplus(step_pre)
    decay_sum = jnp.cumsum(step_size * rate, axis=0)
    sums2 = decay_sum * LOG2E
    log_step = jnp.log2(step_size)
    back2 = sums2 - log_step
    cols = jnp.concatenate(
        [v.reshape(LEN, 6, 4) for v in (sums2, back2, log_step, jnp.zeros_like(sums2))], 2
    ).transpose(1, 0, 2)
    rows = cols.transpose(0, 2, 1)

    pre, act, mixed_y = mix_forward(normed, inner_w, taps, bias, masks, scores, cols, rows)
    gate_pre, grad_gn, stats = gate_forward(
        normed, cot_all, (gate_own, gate_peer), (out_own, out_peer), act, mixed_y, skip, gain
    )
    stats = stats + swap_tensor(stats)
    gate_low, gnormed, grad_y, gain_grad = gate_backward(stats, gate_pre, grad_gn, act, mixed_y, skip, gain)

    def own_tokens(values):
        values = values.astype(BF)
        got = swap_tensor(lax.dynamic_slice_in_dim(values, (1 - t) * 256, 256, 0))
        return lax.dynamic_slice_in_dim(values, t * 256, 256, 0).astype(F32) + got.astype(F32)

    branch = own_tokens(dot_cols(gnormed[:, :768], out_own) + dot_cols(gnormed[:, 768:], out_peer))
    mixed = (hidden.astype(F32) + branch).astype(BF)

    inner_low, sums, flows, grad_scores = mix_backward(
        grad_y, act, mixed_y, pre, scores_t, taps, bias, masks, cols, rows, skip
    )

    grad_scores = grad_scores * visible.T
    grad_scores = (grad_scores + swap_tensor(grad_scores.astype(BF)).astype(F32)).astype(BF)
    grad_c = dot_rows(grad_scores, b_proj)
    grad_b = dot(grad_scores, c_proj)
    bc_grad = jnp.concatenate([grad_b, grad_c], 1) * silu_slope(bc_conv)
    bc_grad_pre = 0.0
    bc_tap_grads = []
    for tap in range(4):
        o = 3 - tap
        part = bc_grad * masks[:, o : o + 1]
        moved = part if o == 0 else jnp.pad(part, ((0, o), (0, 0)))[o:]
        bc_grad_pre = bc_grad_pre + bc_taps[tap] * moved
        bc_tap_grads.append(jnp.sum(part * shifted(bc_pre, o), axis=0))
    bc_tap_grads.append(jnp.sum(bc_grad, axis=0))
    bc_low = bc_grad_pre.astype(BF)

    flows = flows.transpose(1, 0, 2)
    row_flow, col_flow = flows[:, :, :4].reshape(LEN, 24), flows[:, :, 4:].reshape(LEN, 24)
    grad_rate = jnp.cumsum((row_flow - col_flow)[::-1], axis=0)[::-1]
    step_sig = jax.nn.sigmoid(step_pre)
    tiny = step_size < 1e-30
    ratio = jnp.where(tiny, 1.0, step_sig / jnp.where(tiny, 1.0, step_size))
    grad_step_pre = col_flow * ratio + grad_rate * rate * step_sig
    decay_grad = jnp.sum(grad_rate * step_size, axis=0) * rate
    step_bias_grad = jnp.sum(grad_step_pre, axis=0)
    skip_grad = jnp.sum(sums[5].reshape(24, 64), axis=1)
    step_low = grad_step_pre.astype(BF)

    pad_cols = lambda v: jnp.pad(v, ((0, 0), (0, 116)))
    own_tail = jnp.concatenate(
        [jnp.where(c == 0, bc_low[:, :128], bc_low[:, 128:]), pad_cols(step_low[:, :12])], 1
    )
    peer_tail = jnp.concatenate(
        [jnp.where(c == 0, bc_low[:, 128:], bc_low[:, :128]), pad_cols(step_low[:, 12:])], 1
    )
    only_first = jnp.concatenate(
        [jnp.broadcast_to((t == 0).astype(BF), (128,)), jnp.ones((128,), BF)]
    )
    grad_normed = (
        dot_cols(gate_low[:, :768], gate_own)
        + dot_cols(gate_low[:, 768:], gate_peer)
        + dot_cols(inner_low[:, :512], own_a)
        + dot_cols(inner_low[:, 768:1280], peer_a)
        + dot_cols(jnp.concatenate([inner_low[:, 512:768], own_tail * only_first], 1), own_b)
        + dot_cols(jnp.concatenate([inner_low[:, 1280:], peer_tail * only_first], 1), peer_b)
    )
    norm_gain_grad = jnp.sum(grad_normed * resid * norm_scale, axis=0)
    grad_mine = own_tokens(grad_normed)
    mine = hidden.astype(F32)
    scale_mine = lax.dynamic_slice_in_dim(norm_scale, t * 256, 256, 0)
    pre_stat = jnp.sum(grad_mine * norm_gain * mine, axis=-1, keepdims=True)
    grad_hidden = (
        cotangent.astype(F32)
        + scale_mine * norm_gain * grad_mine
        - mine * scale_mine**3 * pre_stat / 1536
    )

    low_own = jnp.concatenate([inner_low[:, :768], own_tail, gate_low[:, :768]], 1)
    low_peer = jnp.concatenate([inner_low[:, 768:], peer_tail, gate_low[:, 768:]], 1)
    part_own = jnp.concatenate([dot_rows(normed, low_own), dot_rows(cot_all, gnormed[:, :768])], 1)
    part_peer = jnp.concatenate([dot_rows(normed, low_peer), dot_rows(cot_all, gnormed[:, 768:])], 1)
    rows_own, rows_peer = reduce_rows(part_own, part_peer, c)

    def halves(start, size):
        mine_cols = rows_own[:, start : start + size]
        other_cols = rows_peer[:, start : start + size]
        return jnp.concatenate(
            [jnp.where(c == 0, mine_cols, other_cols), jnp.where(c == 0, other_cols, mine_cols)], 1
        )

    grad_in = jnp.stack([halves(1024, 768), halves(0, 768)])
    grad_bc = halves(768, 128)
    grad_step = halves(896, 12)
    grad_out = halves(1792, 768).T

    misc = jnp.concatenate(
        [
            jnp.stack(bc_tap_grads).reshape(-1),
            natural(step_bias_grad, 12),
            natural(decay_grad, 12),
            natural(skip_grad, 12),
            jnp.zeros((184,), F32),
        ]
    )
    small = jnp.concatenate(
        [natural(jnp.concatenate([sums[:5], gain_grad], 0), 768), norm_gain_grad[None], misc[None]], 0
    )
    small = reduce_small(small)
    small_other = swap_tensor(small)
    both = jnp.concatenate(
        [jnp.where(t == 0, small, small_other), jnp.where(t == 0, small_other, small)], 1
    )
    bc_sums = small[7, :1280].reshape(5, 256)
    heads = jnp.concatenate([both[7, 1280:1352].reshape(3, 24), both[7, 2816:2888].reshape(3, 24)], 1)
    return (
        mixed,
        grad_hidden,
        small[6] + small_other[6],
        grad_in,
        grad_bc,
        grad_step,
        jnp.concatenate([both[:4], bc_sums[:4]], 1),
        jnp.concatenate([both[4], bc_sums[4]]),
        heads[0],
        heads[1],
        heads[2],
        both[5],
        grad_out,
    )


def solution(mesh):
    return jax.shard_map(
        on_device,
        mesh=mesh,
        in_specs=(
            P(("dp", "tensor"), None),
            P("dp", None),
            P(),
            P(None, "dp", "tensor"),
            P("dp", None),
            P("dp", "tensor"),
            P(),
            P(),
            P(),
            P(),
            P(),
            P(),
            P("tensor", "dp"),
            P(("dp", "tensor"), None),
        ),
        out_specs=(
            P(("dp", "tensor"), None),
            P(("dp", "tensor"), None),
            P(),
            P(None, "dp", "tensor"),
            P("dp", None),
            P("dp", "tensor"),
            P(),
            P(),
            P(),
            P(),
            P(),
            P(),
            P("tensor", "dp"),
        ),
        check_vma=False,
    )
```

time: 1530 us -> 488 us (0.32)
  waiting for transfers between devices: 861 us -> 132 us
  blocking collectives: 217 us -> 0 us
  matrix products: 262 us -> 46.3 us
  starting transfers between devices: 0.44 us -> 132 us
  Pallas kernels: 0 us -> 56 us
  local copies, waits for them, and re-layouts: 104 us -> 66.8 us
    reduce_scatter x5 -> x0, waiting for transfers between devices: 567 us -> none  [the longest x1 218 us: on_device(): lax.psum_scatter(grad_in_part, 'dp', scatter_dimension=1, tiled=True)]
    dot_general x90 -> x18, matrix products: 262 us -> 46.3 us  [the longest x10 29.6 us: dot_cols(): lax.dot_general(left, right, (((1,), (1,)), ((), ())), preferred_element_...]
    all_gather x2 -> x0, blocking collectives: 184 us -> none  [the longest x1 96.9 us: on_device(): lax.all_gather(step_weight, 'dp', axis=0, tiled=True)]
    psum x1 -> x0, waiting for transfers between devices: 149 us -> none  [on_device(): lax.psum((conv_grad, bias_grad, step_bias_grad, decay_grad, skip_grad, ga...]
    unnamed x12 -> x0, waiting for transfers between devices: 145 us -> none
    ppermute x0 -> x49, waiting for transfers between devices: none -> 132 us  [the longest x42 121 us: send(): return lax.ppermute(values, 'dp', pairs)]
    ppermute x0 -> x49, starting transfers between devices: none -> 124 us  [the longest x42 122 us: send(): return lax.ppermute(values, 'dp', pairs)]
    pallas_call x0 -> x4, Pallas kernels: none -> 56 us  [the longest x1 20.8 us: mix_backward(): pl.pallas_call(back_kernel, grid=(6,), in_specs=[block(LEN), block(LEN),...]
  transfers between devices with their start and end apart: 11 -> 50, of which waited for: 7 -> 18; matrix products, arithmetic and copies ran while one was open for 11% -> 23% of each run, Pallas kernels for 0% -> 3%
where the time goes in v1:
time: 488 us; the launch traced here: 478 us
  starting transfers between devices  132 us (27%)
  waiting for transfers between devices  132 us (27%)
  local copies, waits for them, and re-layouts  66.8 us (14%)
  Pallas kernels  56 us (11%)
  matrix products  46.3 us (9%)
  other arithmetic  42.4 us (9%)
    ppermute x42, starting transfers between devices, send(): return lax.ppermute(values, 'dp', pairs)  122 us
    ppermute x42, waiting for transfers between devices, send(): return lax.ppermute(values, 'dp', pairs)  121 us
    dot_general x10, matrix products, dot_cols(): lax.dot_general(left, right, (((1,), (1,)), ((), ())), preferred_element_...  29.6 us
    dynamic_update_slice x28, local copies, waits for them, and re-layouts, place(): lax.dynamic_update_slice(whole, jnp.expand_dims(piece, axis), tuple(start))  23.1 us
    pallas_call x1, Pallas kernels, mix_backward(): pl.pallas_call(back_kernel, grid=(6,), in_specs=[block(LEN), block(LEN),...  20.8 us
    pallas_call x1, Pallas kernels, mix_forward(): pl.pallas_call(mix_kernel, grid=(6,), in_specs=[full(LEN, 1536), pl.Block...  14.3 us
    pallas_call x1, Pallas kernels, gate_forward(): pl.pallas_call(gate_kernel, grid=(6,), in_specs=[full(LEN, 1536), full(LE...  12.4 us
    dot_general x5, matrix products, dot_rows(): lax.dot_general(left, right, (((0,), (0,)), ((), ())), preferred_element_...  12.4 us
  transfers between devices with their start and end apart: 50, of which 18 were waited for; matrix products, arithmetic and copies ran while one was open for 23% of the time, Pallas kernels for 3%

profile of v1, /device:TPU:25, one launch (start us, length us, event | category | flops | bytes accessed | tf_op | source)
XLA Modules:
  0.0 478.4 jit_solution(2071204809831745176)
XLA Ops:
  12.5 3.7 collective-permute-start.19
  16.3 25.2 %collective-permute-done.19 = bf16[48,1024]{1,0:T(8,128)(2,1)S(1)} collective-permute-done((bf16[48,1024]{1,0:T(8,128)(2,1)S(1)}, bf16[48,1024]{1,0:T(8,128)(2,1)S(1)}, u32[]{:S(2)}, u32[]{:S(2)}) %collective-permute-start.19) | collective-permute-done | bytes 98336 | tf_op jit(solution)/shard_map/ppermute | solution.py:42
  45.0 2.7 collective-permute-start.28
  62.6 2.0 collective-permute-done.5
  72.2 2.0 collective-permute-start.31
  79.2 4.7 collective-permute-done.30
  88.8 2.1 collective-permute-done.24
  93.6 2.3 collective-permute-start.9
  97.6 23.4 %collective-permute-start.33 = (bf16[4,2,4,48,512]{4,3,2,1,0:T(8,128)(2,1)}, bf16[4,2,4,48,512]{4,3,2,1,0:T(8,128)(2,1)}, u32[]{:S(2)}, u32[]{:S(2)}) collective-permute-start(bf16[4,2,4,48,512]{4,3,2,1,0:T(8,128)(2,1)} %bitcast_dynamic-update-slice_fusion.11), channel_id=1, source_target_pairs={{0,2},{2,0},{4,6},{6,4},{8,10},{10,8},{12,14},{14,12},{16,18},{18,... | collective-permute-start | bytes 4718600 | tf_op jit(solution)/shard_map/ppermute | solution.py:42
  122.4 2.3 fusion.37
  135.1 3.4 collective-permute-start.32
  144.7 13.1 %collective-permute-done.16 = bf16[4,2,48,768]{3,2,1,0:T(8,128)(2,1)S(1)} collective-permute-done((bf16[4,2,48,768]{3,2,1,0:T(8,128)(2,1)}, bf16[4,2,48,768]{3,2,1,0:T(8,128)(2,1)S(1)}, u32[]{:S(2)}, u32[]{:S(2)}) %collective-permute-start.16) | collective-permute-done | bytes 589856 | tf_op jit(solution)/shard_map/ppermute | solution.py:42
  169.5 14.3 %mix_forward.1 = (f32[512,1536]{1,0:T(8,128)}, bf16[512,1536]{1,0:T(8,128)(2,1)S(1)}, f32[512,1536]{1,0:T(8,128)}) custom-call(bf16[512,1536]{1,0:T(8,128)(2,1)} %copy-done, bf16[1536,512]{1,0:T(8,128)(2,1)} %bitcast.46.own_a, bf16[1536,512]{1,0:T(8,128)(2,1)} %bitcast.58.own_b, bf16[1536,512]{1,0:T(8,128)(2,1)} %bitcast.59.peer_a, ...), custom_call_target="tpu_custom_call" | custom-call | flops 4000000000 | bytes 16000000 | tf_op jit(solution)/shard_map/mix_forward/pallas_call | solution.py:181
  185.0 12.4 %gate_forward.1 = (f32[512,1536]{1,0:T(8,128)}, f32[512,1536]{1,0:T(8,128)}, f32[8,512]{1,0:T(8,128)S(1)}) custom-call(bf16[512,1536]{1,0:T(8,128)(2,1)S(1)} %copy-done.1, bf16[512,1536]{1,0:T(8,128)(2,1)S(1)} %pad_maximum_fusion.2.cot, bf16[1536,768]{1,0:T(8,128)(2,1)} %bitcast.196, bf16[1536,768]{1,0:T(8,128)(2,1)} %bitcast.17.gate_peer, ...), custom_call_target="tpu_custom_call" | custom-call | flops 4899999744 | bytes 24000000 | tf_op jit(solution)/shard_map/gate_forward/pallas_call | solution.py:243
  197.9 2.3 collective-permute-done.34
  200.2 8.5 %gate_backward.1 = (bf16[512,1536]{1,0:T(8,128)(2,1)S(1)}, bf16[512,1536]{1,0:T(8,128)(2,1)S(1)}, f32[512,1536]{1,0:T(8,128)}, f32[1,1536]{1,0:T(1,128)S(1)}) custom-call(f32[8,512]{1,0:T(8,128)S(1)} %add.418.stats, f32[512,1536]{1,0:T(8,128)} %get-tuple-element.30.gate_pre, f32[512,1536]{1,0:T(8,128)} %get-tuple-element.31.grad_gn, ...), custom_call_target="tpu_custom_call" | custom-call | flops 20000000 | bytes 18000000 | tf_op jit(solution)/shard_map/gate_backward/pallas_call | solution.py:287
  209.8 20.8 %mix_backward.1 = (bf16[512,1536]{1,0:T(8,128)(2,1)}, f32[8,1536]{1,0:T(8,128)S(1)}, f32[6,512,8]{2,1,0:T(8,128)}, f32[512,512]{1,0:T(8,128)S(1)}) custom-call(f32[512,1536]{1,0:T(8,128)} %get-tuple-element.34.grad_y, bf16[512,1536]{1,0:T(8,128)(2,1)} %copy-done.5, f32[512,1536]{1,0:T(8,128)} %get-tuple-element.28.mixed, f32[512,1536]{1,0:T(8,128)} %get-tuple-element.35.pre, ...), custom_call_target="tpu_custom_call" | custom-call | flops 4000000000 | bytes 14000000 | tf_op jit(solution)/shard_map/mix_backward/pallas_call | solution.py:377
  230.6 4.2 fusion.110
  248.4 2.8 convolution_convert_fusion.1
  251.2 6.1 %collective-permute-done.36 = bf16[512,512]{1,0:T(8,128)(2,1)S(1)} collective-permute-done((bf16[512,512]{1,0:T(8,128)(2,1)S(1)}, bf16[512,512]{1,0:T(8,128)(2,1)S(1)}, u32[]{:S(2)}, u32[]{:S(2)}) %collective-permute-start.36) | collective-permute-done | bytes 524320 | tf_op jit(solution)/shard_map/ppermute | solution.py:46
  259.9 4.8 %convolution_convert_fusion = bf16[1536,1792]{1,0:T(8,128)(2,1)} fusion(bf16[512,1536]{1,0:T(8,128)(2,1)S(1)} %copy-done.1, bf16[512,768]{1,0:T(8,128)(2,1)S(1)} %get-tuple-element.66, bf16[512,128]{1,0:T(8,128)(2,1)S(1)} %pad.57, bf16[512,128]{1,0:T(8,128)(2,1)S(1)} %get-tuple-element.94, bf16[512,768]{1,0:T(8,128)(2,1)S(1)} %get-tuple-element.64), kind=kOutput, calls=%fused_computation.4 | convolution fusion | flops 2828664832 | bytes 8912896 | tf_op jit(solution)/shard_map/dot_general | solution.py:105
  264.7 7.2 %pad_maximum_fusion = bf16[1536,2560]{1,0:T(8,128)(2,1)} fusion(bf16[1536,768]{1,0:T(8,128)(2,1)} %convolution_convert_fusion.1, bf16[1536,1792]{1,0:T(8,128)(2,1)} %convolution_convert_fusion), kind=kLoop, calls=%fused_computation.3 | loop fusion | flops 15728640 | bytes 15728640 | tf_op jit(solution)/shard_map/concatenate | solution.py:609
  271.9 2.3 collective-permute-start.47
  277.4 4.1 fusion.60
  281.4 4.2 fusion.62
  287.1 4.9 %fusion.99 = f32[512,1536]{1,0:T(8,128)} fusion(bf16[1536,768]{1,0:T(8,128)(2,1)} %bitcast.17.gate_peer, bf16[512,1536]{1,0:T(8,128)(2,1)S(1)} %copy-done.4), kind=kOutput, calls=%fused_computation.281 | convolution fusion | flops 1207959552 | bytes 6291456 | tf_op jit(solution)/shard_map/dot_general | solution.py:109
  292.1 3.1 fusion.11
  295.1 7.3 %fusion = bf16[1536,2560]{1,0:T(8,128)(2,1)} fusion(f32[1536,768]{1,0:T(8,128)S(1)} %fusion.42, f32[1536,1792]{1,0:T(8,128)S(1)} %fusion.11, bf16[1536,2560]{1,0:T(8,128)(2,1)} %collective-permute-done.47), kind=kLoop, calls=%fused_computation.1 | loop fusion | flops 15728640 | bytes 31457280 | tf_op jit(solution)/shard_map/convert_element_type | solution.py:83
  302.5 7.3 %all-to-all-start = ((bf16[32,48,2560]{2,1,0:T(8,128)(2,1)}), bf16[32,48,2560]{2,1,0:T(8,128)(2,1)}, u32[]{:S(2)}, u32[]{:S(2)}) async-start(bf16[32,48,2560]{2,1,0:T(8,128)(2,1)} %bitcast.195), calls=%async_computation | async-start | bytes 15728640 | tf_op jit(solution)/shard_map/all_to_all | solution.py:84
  310.2 2.6 fusion.56
  312.8 2.6 fusion.52
  315.6 4.4 fusion.9
  320.8 3.1 fusion.40
  323.9 3.0 collective-permute-start.39
  327.0 3.1 fusion.10
  330.1 9.5 %collective-permute-done.39 = f32[8,1536]{1,0:T(8,128)S(1)} collective-permute-done((f32[8,1536]{1,0:T(8,128)S(1)}, f32[8,1536]{1,0:T(8,128)S(1)}, u32[]{:S(2)}, u32[]{:S(2)}) %collective-permute-start.39) | collective-permute-done | bytes 49184 | tf_op jit(solution)/shard_map/ppermute | solution.py:42
  339.6 9.8 %collective-permute-start.41 = (f32[8,1536]{1,0:T(8,128)S(1)}, f32[8,1536]{1,0:T(8,128)S(1)}, u32[]{:S(2)}, u32[]{:S(2)}) collective-permute-start(f32[8,1536]{1,0:T(8,128)S(1)} %add.439), channel_id=1, source_target_pairs={{0,4},{2,6},{4,8},{6,10},{8,12},{10,14},{12,0},{14,2},{16,20},{18,... | collective-permute-start | bytes 147464 | tf_op jit(solution)/shard_map/ppermute | solution.py:42
  349.4 30.8 %collective-permute-start.42 = (f32[8,1536]{1,0:T(8,128)S(1)}, f32[8,1536]{1,0:T(8,128)S(1)}, u32[]{:S(2)}, u32[]{:S(2)}) collective-permute-start(f32[8,1536]{1,0:T(8,128)S(1)} %add.439), channel_id=1, source_target_pairs={{0,12},{2,14},{4,0},{6,2},{8,4},{10,6},{12,8},{14,10},{16,28},{18,... | collective-permute-start | bytes 147464 | tf_op jit(solution)/shard_map/ppermute | solution.py:42
  383.1 5.8 %collective-permute-done.42 = f32[8,1536]{1,0:T(8,128)S(1)} collective-permute-done((f32[8,1536]{1,0:T(8,128)S(1)}, f32[8,1536]{1,0:T(8,128)S(1)}, u32[]{:S(2)}, u32[]{:S(2)}) %collective-permute-start.42) | collective-permute-done | bytes 49184 | tf_op jit(solution)/shard_map/ppermute | solution.py:42
  388.9 9.7 %collective-permute-done.40 = f32[8,1536]{1,0:T(8,128)S(1)} collective-permute-done((f32[8,1536]{1,0:T(8,128)S(1)}, f32[8,1536]{1,0:T(8,128)S(1)}, u32[]{:S(2)}, u32[]{:S(2)}) %collective-permute-start.40) | collective-permute-done | bytes 49184 | tf_op jit(solution)/shard_map/ppermute | solution.py:42
  398.6 5.4 %collective-permute-start.44 = (f32[8,1536]{1,0:T(8,128)S(1)}, f32[8,1536]{1,0:T(8,128)S(1)}, u32[]{:S(2)}, u32[]{:S(2)}) collective-permute-start(f32[8,1536]{1,0:T(8,128)S(1)} %add_add_fusion.1), channel_id=1, source_target_pairs={{0,32},{2,34},{4,36},{6,38},{8,40},{10,42},{12,44},{14,46},{16,48}... | collective-permute-start | bytes 147464 | tf_op jit(solution)/shard_map/ppermute | solution.py:42
  404.0 4.2 collective-permute-start.45
  410.3 34.2 %collective-permute-done.44 = f32[8,1536]{1,0:T(8,128)S(1)} collective-permute-done((f32[8,1536]{1,0:T(8,128)S(1)}, f32[8,1536]{1,0:T(8,128)S(1)}, u32[]{:S(2)}, u32[]{:S(2)}) %collective-permute-start.44) | collective-permute-done | bytes 49184 | tf_op jit(solution)/shard_map/ppermute | solution.py:42
  444.5 12.0 %collective-permute-done.43 = f32[8,1536]{1,0:T(8,128)S(1)} collective-permute-done((f32[8,1536]{1,0:T(8,128)S(1)}, f32[8,1536]{1,0:T(8,128)S(1)}, u32[]{:S(2)}, u32[]{:S(2)}) %collective-permute-start.43) | collective-permute-done | bytes 49184 | tf_op jit(solution)/shard_map/ppermute | solution.py:42
  456.7 2.9 collective-permute-done.46
  464.2 4.7 convert_reduce_fusion
  469.0 2.7 collective-permute-start.48
  471.7 3.5 fusion.29
  (435 shorter events, 118.3 us)
Async XLA Ops:
  0.7 96.0 %collective-permute-start.1 = (bf16[256,1536]{1,0:T(8,128)(2,1)}, bf16[256,1536]{1,0:T(8,128)(2,1)S(1)}, u32[]{:S(2)}, u32[]{:S(2)}) collective-permute-start(bf16[256,1536]{1,0:T(8,128)(2,1)} %param.27), channel_id=1, source_target_pairs={{0,1},{1,0},{2,3},{3,2},{4,5},{5,4},{6,7},{7,6},{8,9},{9,8},{10,11... | collective-permute-start | bytes 2359304 | tf_op jit(solution)/shard_map/ppermute | solution.py:46
  2.4 95.2 %collective-permute-start = (bf16[256,1536]{1,0:T(8,128)(2,1)}, bf16[256,1536]{1,0:T(8,128)(2,1)S(1)}, u32[]{:S(2)}, u32[]{:S(2)}) collective-permute-start(bf16[256,1536]{1,0:T(8,128)(2,1)} %param.14), channel_id=1, source_target_pairs={{0,1},{1,0},{2,3},{3,2},{4,5},{5,4},{6,7},{7,6},{8,9},{9,8},{10,11... | collective-permute-start | bytes 2359304 | tf_op jit(solution)/shard_map/ppermute | solution.py:46
  5.1 7.3 %collective-permute-start.18 = (bf16[24,1024]{1,0:T(8,128)(2,1)S(1)}, bf16[24,1024]{1,0:T(8,128)(2,1)S(1)}, u32[]{:S(2)}, u32[]{:S(2)}) collective-permute-start(bf16[24,1024]{1,0:T(8,128)(2,1)S(1)} %constant_dynamic-slice_fusion.5), channel_id=1, source_target_pairs={{0,2},{2,0},{4,6},{6,4},{8,10},{10,8},{12,14},{14,12},{16,18},{18,... | collective-permute-start | bytes 147464 | tf_op jit(solution)/shard_map/ppermute | solution.py:42
  7.0 9.2 %collective-permute-start.2 = (bf16[24,1536]{1,0:T(8,128)(2,1)S(1)}, bf16[24,1536]{1,0:T(8,128)(2,1)S(1)}, u32[]{:S(2)}, u32[]{:S(2)}) collective-permute-start(bf16[24,1536]{1,0:T(8,128)(2,1)S(1)} %constant_dynamic-slice_fusion.6), channel_id=1, source_target_pairs={{0,2},{2,0},{4,6},{6,4},{8,10},{10,8},{12,14},{14,12},{16,18},{18,... | collective-permute-start | bytes 221192 | tf_op jit(solution)/shard_map/ppermute | solution.py:42
  12.5 29.0 %collective-permute-start.19 = (bf16[48,1024]{1,0:T(8,128)(2,1)S(1)}, bf16[48,1024]{1,0:T(8,128)(2,1)S(1)}, u32[]{:S(2)}, u32[]{:S(2)}) collective-permute-start(bf16[48,1024]{1,0:T(8,128)(2,1)S(1)} %pad_maximum_fusion.10), channel_id=1, source_target_pairs={{0,16},{2,18},{4,20},{6,22},{8,24},{10,26},{12,28},{14,30},{16,0},... | collective-permute-start | bytes 294920 | tf_op jit(solution)/shard_map/ppermute | solution.py:42
  16.2 28.8 %collective-permute-start.3 = (bf16[48,1536]{1,0:T(8,128)(2,1)S(1)}, bf16[48,1536]{1,0:T(8,128)(2,1)S(1)}, u32[]{:S(2)}, u32[]{:S(2)}) collective-permute-start(bf16[48,1536]{1,0:T(8,128)(2,1)S(1)} %pad_maximum_fusion.8), channel_id=1, source_target_pairs={{0,16},{2,18},{4,20},{6,22},{8,24},{10,26},{12,28},{14,30},{16,0},... | collective-permute-start | bytes 442376 | tf_op jit(solution)/shard_map/ppermute | solution.py:42
  41.6 9.4 %collective-permute-start.26 = (bf16[2,48,512]{2,1,0:T(8,128)(2,1)S(1)}, bf16[2,48,512]{2,1,0:T(8,128)(2,1)S(1)}, u32[]{:S(2)}, u32[]{:S(2)}) collective-permute-start(bf16[2,48,512]{2,1,0:T(8,128)(2,1)S(1)} %get-tuple-element.55), channel_id=1, source_target_pairs={{0,32},{2,34},{4,36},{6,38},{8,40},{10,42},{12,44},{14,46},{16,48}... | collective-permute-start | bytes 294920 | tf_op jit(solution)/shard_map/ppermute | solution.py:42
  42.9 8.1 %collective-permute-start.27 = (bf16[2,48,512]{2,1,0:T(8,128)(2,1)S(1)}, bf16[2,48,512]{2,1,0:T(8,128)(2,1)S(1)}, u32[]{:S(2)}, u32[]{:S(2)}) collective-permute-start(bf16[2,48,512]{2,1,0:T(8,128)(2,1)S(1)} %get-tuple-element.55), channel_id=1, source_target_pairs={{0,96},{2,98},{4,100},{6,102},{8,104},{10,106},{12,108},{14,110},{... | collective-permute-start | bytes 294920 | tf_op jit(solution)/shard_map/ppermute | solution.py:42
  45.0 7.6 %collective-permute-start.28 = (bf16[2,48,512]{2,1,0:T(8,128)(2,1)S(1)}, bf16[2,48,512]{2,1,0:T(8,128)(2,1)S(1)}, u32[]{:S(2)}, u32[]{:S(2)}) collective-permute-start(bf16[2,48,512]{2,1,0:T(8,128)(2,1)S(1)} %get-tuple-element.55), channel_id=1, source_target_pairs={{0,64},{2,66},{4,68},{6,70},{8,72},{10,74},{12,76},{14,78},{16,80}... | collective-permute-start | bytes 294920 | tf_op jit(solution)/shard_map/ppermute | solution.py:42
  51.0 4.7 collective-permute-start.20
  51.1 6.6 %collective-permute-start.21 = (bf16[2,48,512]{2,1,0:T(8,128)(2,1)S(1)}, bf16[2,48,512]{2,1,0:T(8,128)(2,1)S(1)}, u32[]{:S(2)}, u32[]{:S(2)}) collective-permute-start(bf16[2,48,512]{2,1,0:T(8,128)(2,1)S(1)} %get-tuple-element.57), channel_id=1, source_target_pairs={{0,12},{2,14},{4,0},{6,2},{8,4},{10,6},{12,8},{14,10},{16,28},{18,... | collective-permute-start | bytes 294920 | tf_op jit(solution)/shard_map/ppermute | solution.py:42
  52.6 5.4 %collective-permute-start.22 = (bf16[2,48,512]{2,1,0:T(8,128)(2,1)S(1)}, bf16[2,48,512]{2,1,0:T(8,128)(2,1)S(1)}, u32[]{:S(2)}, u32[]{:S(2)}) collective-permute-start(bf16[2,48,512]{2,1,0:T(8,128)(2,1)S(1)} %get-tuple-element.57), channel_id=1, source_target_pairs={{0,8},{2,10},{4,12},{6,14},{8,0},{10,2},{12,4},{14,6},{16,24},{18,... | collective-permute-start | bytes 294920 | tf_op jit(solution)/shard_map/ppermute | solution.py:42
  55.8 5.8 %collective-permute-start.4 = (bf16[2,48,768]{2,1,0:T(8,128)(2,1)S(1)}, bf16[2,48,768]{2,1,0:T(8,128)(2,1)S(1)}, u32[]{:S(2)}, u32[]{:S(2)}) collective-permute-start(bf16[2,48,768]{2,1,0:T(8,128)(2,1)S(1)} %get-tuple-element.59), channel_id=1, source_target_pairs={{0,4},{2,6},{4,8},{6,10},{8,12},{10,14},{12,0},{14,2},{16,20},{18,... | collective-permute-start | bytes 442376 | tf_op jit(solution)/shard_map/ppermute | solution.py:42
  57.7 6.9 %collective-permute-start.5 = (bf16[2,48,768]{2,1,0:T(8,128)(2,1)S(1)}, bf16[2,48,768]{2,1,0:T(8,128)(2,1)S(1)}, u32[]{:S(2)}, u32[]{:S(2)}) collective-permute-start(bf16[2,48,768]{2,1,0:T(8,128)(2,1)S(1)} %get-tuple-element.59), channel_id=1, source_target_pairs={{0,12},{2,14},{4,0},{6,2},{8,4},{10,6},{12,8},{14,10},{16,28},{18,... | collective-permute-start | bytes 442376 | tf_op jit(solution)/shard_map/ppermute | solution.py:42
  58.0 8.2 %collective-permute-start.6 = (bf16[2,48,768]{2,1,0:T(8,128)(2,1)S(1)}, bf16[2,48,768]{2,1,0:T(8,128)(2,1)S(1)}, u32[]{:S(2)}, u32[]{:S(2)}) collective-permute-start(bf16[2,48,768]{2,1,0:T(8,128)(2,1)S(1)} %get-tuple-element.59), channel_id=1, source_target_pairs={{0,8},{2,10},{4,12},{6,14},{8,0},{10,2},{12,4},{14,6},{16,24},{18,... | collective-permute-start | bytes 442376 | tf_op jit(solution)/shard_map/ppermute | solution.py:42
  61.6 7.8 %collective-permute-start.11 = (bf16[2,48,768]{2,1,0:T(8,128)(2,1)S(1)}, bf16[2,48,768]{2,1,0:T(8,128)(2,1)S(1)}, u32[]{:S(2)}, u32[]{:S(2)}) collective-permute-start(bf16[2,48,768]{2,1,0:T(8,128)(2,1)S(1)} %get-tuple-element.61), channel_id=1, source_target_pairs={{0,32},{2,34},{4,36},{6,38},{8,40},{10,42},{12,44},{14,46},{16,48}... | collective-permute-start | bytes 442376 | tf_op jit(solution)/shard_map/ppermute | solution.py:42
  64.6 6.2 %collective-permute-start.12 = (bf16[2,48,768]{2,1,0:T(8,128)(2,1)S(1)}, bf16[2,48,768]{2,1,0:T(8,128)(2,1)S(1)}, u32[]{:S(2)}, u32[]{:S(2)}) collective-permute-start(bf16[2,48,768]{2,1,0:T(8,128)(2,1)S(1)} %get-tuple-element.61), channel_id=1, source_target_pairs={{0,96},{2,98},{4,100},{6,102},{8,104},{10,106},{12,108},{14,110},{... | collective-permute-start | bytes 442376 | tf_op jit(solution)/shard_map/ppermute | solution.py:42
  66.1 6.1 %collective-permute-start.13 = (bf16[2,48,768]{2,1,0:T(8,128)(2,1)S(1)}, bf16[2,48,768]{2,1,0:T(8,128)(2,1)S(1)}, u32[]{:S(2)}, u32[]{:S(2)}) collective-permute-start(bf16[2,48,768]{2,1,0:T(8,128)(2,1)S(1)} %get-tuple-element.61), channel_id=1, source_target_pairs={{0,64},{2,66},{4,68},{6,70},{8,72},{10,74},{12,76},{14,78},{16,80}... | collective-permute-start | bytes 442376 | tf_op jit(solution)/shard_map/ppermute | solution.py:42
  69.4 9.1 %collective-permute-start.29 = (bf16[4,2,48,512]{3,2,1,0:T(8,128)(2,1)S(1)}, bf16[4,2,48,512]{3,2,1,0:T(8,128)(2,1)S(1)}, u32[]{:S(2)}, u32[]{:S(2)}) collective-permute-start(bf16[4,2,48,512]{3,2,1,0:T(8,128)(2,1)S(1)} %bitcast_dynamic-update-slice_fusion.28), channel_id=1, source_target_pairs={{0,4},{2,6},{4,8},{6,10},{8,12},{10,14},{12,0},{14,2},{16,20},{18,... | collective-permute-start | bytes 1179656 | tf_op jit(solution)/shard_map/ppermute | solution.py:42
  70.8 13.1 %collective-permute-start.30 = (bf16[4,2,48,512]{3,2,1,0:T(8,128)(2,1)S(1)}, bf16[4,2,48,512]{3,2,1,0:T(8,128)(2,1)S(1)}, u32[]{:S(2)}, u32[]{:S(2)}) collective-permute-start(bf16[4,2,48,512]{3,2,1,0:T(8,128)(2,1)S(1)} %bitcast_dynamic-update-slice_fusion.28), channel_id=1, source_target_pairs={{0,12},{2,14},{4,0},{6,2},{8,4},{10,6},{12,8},{14,10},{16,28},{18,... | collective-permute-start | bytes 1179656 | tf_op jit(solution)/shard_map/ppermute | solution.py:42
  72.2 12.6 %collective-permute-start.31 = (bf16[4,2,48,512]{3,2,1,0:T(8,128)(2,1)S(1)}, bf16[4,2,48,512]{3,2,1,0:T(8,128)(2,1)S(1)}, u32[]{:S(2)}, u32[]{:S(2)}) collective-permute-start(bf16[4,2,48,512]{3,2,1,0:T(8,128)(2,1)S(1)} %bitcast_dynamic-update-slice_fusion.28), channel_id=1, source_target_pairs={{0,8},{2,10},{4,12},{6,14},{8,0},{10,2},{12,4},{14,6},{16,24},{18,... | collective-permute-start | bytes 1179656 | tf_op jit(solution)/shard_map/ppermute | solution.py:42
  78.4 9.0 %collective-permute-start.23 = (bf16[2,4,48,512]{3,2,1,0:T(8,128)(2,1)S(1)}, bf16[2,4,48,512]{3,2,1,0:T(8,128)(2,1)S(1)}, u32[]{:S(2)}, u32[]{:S(2)}) collective-permute-start(bf16[2,4,48,512]{3,2,1,0:T(8,128)(2,1)S(1)} %bitcast_dynamic-update-slice_fusion.24), channel_id=1, source_target_pairs={{0,32},{2,34},{4,36},{6,38},{8,40},{10,42},{12,44},{14,46},{16,48}... | collective-permute-start | bytes 1179656 | tf_op jit(solution)/shard_map/ppermute | solution.py:42
  83.9 6.9 %collective-permute-start.24 = (bf16[2,4,48,512]{3,2,1,0:T(8,128)(2,1)S(1)}, bf16[2,4,48,512]{3,2,1,0:T(8,128)(2,1)S(1)}, u32[]{:S(2)}, u32[]{:S(2)}) collective-permute-start(bf16[2,4,48,512]{3,2,1,0:T(8,128)(2,1)S(1)} %bitcast_dynamic-update-slice_fusion.24), channel_id=1, source_target_pairs={{0,96},{2,98},{4,100},{6,102},{8,104},{10,106},{12,108},{14,110},{... | collective-permute-start | bytes 1179656 | tf_op jit(solution)/shard_map/ppermute | solution.py:42
  84.8 8.8 %collective-permute-start.25 = (bf16[2,4,48,512]{3,2,1,0:T(8,128)(2,1)S(1)}, bf16[2,4,48,512]{3,2,1,0:T(8,128)(2,1)S(1)}, u32[]{:S(2)}, u32[]{:S(2)}) collective-permute-start(bf16[2,4,48,512]{3,2,1,0:T(8,128)(2,1)S(1)} %bitcast_dynamic-update-slice_fusion.24), channel_id=1, source_target_pairs={{0,64},{2,66},{4,68},{6,70},{8,72},{10,74},{12,76},{14,78},{16,80}... | collective-permute-start | bytes 1179656 | tf_op jit(solution)/shard_map/ppermute | solution.py:42
  87.4 40.0 %collective-permute-start.7 = (bf16[2,4,48,768]{3,2,1,0:T(8,128)(2,1)}, bf16[2,4,48,768]{3,2,1,0:T(8,128)(2,1)}, u32[]{:S(2)}, u32[]{:S(2)}) collective-permute-start(bf16[2,4,48,768]{3,2,1,0:T(8,128)(2,1)} %bitcast_dynamic-update-slice_fusion.16), channel_id=1, source_target_pairs={{0,32},{2,34},{4,36},{6,38},{8,40},{10,42},{12,44},{14,46},{16,48}... | collective-permute-start | bytes 1769480 | tf_op jit(solution)/shard_map/ppermute | solution.py:42
  90.9 40.3 %collective-permute-start.8 = (bf16[2,4,48,768]{3,2,1,0:T(8,128)(2,1)}, bf16[2,4,48,768]{3,2,1,0:T(8,128)(2,1)}, u32[]{:S(2)}, u32[]{:S(2)}) collective-permute-start(bf16[2,4,48,768]{3,2,1,0:T(8,128)(2,1)} %bitcast_dynamic-update-slice_fusion.16), channel_id=1, source_target_pairs={{0,96},{2,98},{4,100},{6,102},{8,104},{10,106},{12,108},{14,110},{... | collective-permute-start | bytes 1769480 | tf_op jit(solution)/shard_map/ppermute | solution.py:42
  93.6 41.5 %collective-permute-start.9 = (bf16[2,4,48,768]{3,2,1,0:T(8,128)(2,1)}, bf16[2,4,48,768]{3,2,1,0:T(8,128)(2,1)}, u32[]{:S(2)}, u32[]{:S(2)}) collective-permute-start(bf16[2,4,48,768]{3,2,1,0:T(8,128)(2,1)} %bitcast_dynamic-update-slice_fusion.16), channel_id=1, source_target_pairs={{0,64},{2,66},{4,68},{6,70},{8,72},{10,74},{12,76},{14,78},{16,80}... | collective-permute-start | bytes 1769480 | tf_op jit(solution)/shard_map/ppermute | solution.py:42
  96.7 43.7 %collective-permute-start.14 = (bf16[4,2,48,768]{3,2,1,0:T(8,128)(2,1)}, bf16[4,2,48,768]{3,2,1,0:T(8,128)(2,1)}, u32[]{:S(2)}, u32[]{:S(2)}) collective-permute-start(bf16[4,2,48,768]{3,2,1,0:T(8,128)(2,1)} %bitcast_dynamic-update-slice_fusion.20), channel_id=1, source_target_pairs={{0,4},{2,6},{4,8},{6,10},{8,12},{10,14},{12,0},{14,2},{16,20},{18,... | collective-permute-start | bytes 1769480 | tf_op jit(solution)/shard_map/ppermute | solution.py:42
  97.6 61.7 %collective-permute-start.33 = (bf16[4,2,4,48,512]{4,3,2,1,0:T(8,128)(2,1)}, bf16[4,2,4,48,512]{4,3,2,1,0:T(8,128)(2,1)}, u32[]{:S(2)}, u32[]{:S(2)}) collective-permute-start(bf16[4,2,4,48,512]{4,3,2,1,0:T(8,128)(2,1)} %bitcast_dynamic-update-slice_fusion.11), channel_id=1, source_target_pairs={{0,2},{2,0},{4,6},{6,4},{8,10},{10,8},{12,14},{14,12},{16,18},{18,... | collective-permute-start | bytes 4718600 | tf_op jit(solution)/shard_map/ppermute | solution.py:42
  127.4 16.4 %collective-permute-start.15 = (bf16[4,2,48,768]{3,2,1,0:T(8,128)(2,1)}, bf16[4,2,48,768]{3,2,1,0:T(8,128)(2,1)S(1)}, u32[]{:S(2)}, u32[]{:S(2)}) collective-permute-start(bf16[4,2,48,768]{3,2,1,0:T(8,128)(2,1)} %bitcast_dynamic-update-slice_fusion.20), channel_id=1, source_target_pairs={{0,12},{2,14},{4,0},{6,2},{8,4},{10,6},{12,8},{14,10},{16,28},{18,... | collective-permute-start | bytes 1769480 | tf_op jit(solution)/shard_map/ppermute | solution.py:42
  131.2 26.6 %collective-permute-start.16 = (bf16[4,2,48,768]{3,2,1,0:T(8,128)(2,1)}, bf16[4,2,48,768]{3,2,1,0:T(8,128)(2,1)S(1)}, u32[]{:S(2)}, u32[]{:S(2)}) collective-permute-start(bf16[4,2,48,768]{3,2,1,0:T(8,128)(2,1)} %bitcast_dynamic-update-slice_fusion.20), channel_id=1, source_target_pairs={{0,8},{2,10},{4,12},{6,14},{8,0},{10,2},{12,4},{14,6},{16,24},{18,... | collective-permute-start | bytes 1769480 | tf_op jit(solution)/shard_map/ppermute | solution.py:42
  135.1 34.3 %collective-permute-start.32 = (bf16[4,2,4,48,512]{4,3,2,1,0:T(8,128)(2,1)}, bf16[4,2,4,48,512]{4,3,2,1,0:T(8,128)(2,1)}, u32[]{:S(2)}, u32[]{:S(2)}) collective-permute-start(bf16[4,2,4,48,512]{4,3,2,1,0:T(8,128)(2,1)} %bitcast_dynamic-update-slice_fusion.12), channel_id=1, source_target_pairs={{0,2},{2,0},{4,6},{6,4},{8,10},{10,8},{12,14},{14,12},{16,18},{18,... | collective-permute-start | bytes 4718600 | tf_op jit(solution)/shard_map/ppermute | solution.py:42
  140.5 44.5 %collective-permute-start.10 = (bf16[4,2,4,48,768]{4,3,2,1,0:T(8,128)(2,1)}, bf16[4,2,4,48,768]{4,3,2,1,0:T(8,128)(2,1)}, u32[]{:S(2)}, u32[]{:S(2)}) collective-permute-start(bf16[4,2,4,48,768]{4,3,2,1,0:T(8,128)(2,1)} %bitcast_dynamic-update-slice_fusion.4), channel_id=1, source_target_pairs={{0,2},{2,0},{4,6},{6,4},{8,10},{10,8},{12,14},{14,12},{16,18},{18,... | collective-permute-start | bytes 7077896 | tf_op jit(solution)/shard_map/ppermute | solution.py:42
  158.6 26.4 %collective-permute-start.17 = (bf16[4,2,4,48,768]{4,3,2,1,0:T(8,128)(2,1)}, bf16[4,2,4,48,768]{4,3,2,1,0:T(8,128)(2,1)}, u32[]{:S(2)}, u32[]{:S(2)}) collective-permute-start(bf16[4,2,4,48,768]{4,3,2,1,0:T(8,128)(2,1)} %bitcast_dynamic-update-slice_fusion.3), channel_id=1, source_target_pairs={{0,2},{2,0},{4,6},{6,4},{8,10},{10,8},{12,14},{14,12},{16,18},{18,... | collective-permute-start | bytes 7077896 | tf_op jit(solution)/shard_map/ppermute | solution.py:42
  244.9 12.3 %collective-permute-start.36 = (bf16[512,512]{1,0:T(8,128)(2,1)S(1)}, bf16[512,512]{1,0:T(8,128)(2,1)S(1)}, u32[]{:S(2)}, u32[]{:S(2)}) collective-permute-start(bf16[512,512]{1,0:T(8,128)(2,1)S(1)} %fusion.34), channel_id=1, source_target_pairs={{0,1},{1,0},{2,3},{3,2},{4,5},{5,4},{6,7},{7,6},{8,9},{9,8},{10,11... | collective-permute-start | bytes 1572872 | tf_op jit(solution)/shard_map/ppermute | solution.py:46
  271.9 23.3 %collective-permute-start.47 = (bf16[1536,2560]{1,0:T(8,128)(2,1)}, bf16[1536,2560]{1,0:T(8,128)(2,1)}, u32[]{:S(2)}, u32[]{:S(2)}) collective-permute-start(bf16[1536,2560]{1,0:T(8,128)(2,1)} %pad_maximum_fusion), channel_id=1, source_target_pairs={{0,2},{2,0},{4,6},{6,4},{8,10},{10,8},{12,14},{14,12},{16,18},{18,... | collective-permute-start | bytes 23592968 | tf_op jit(solution)/shard_map/ppermute | solution.py:42
  302.5 161.7 %all-to-all-start = ((bf16[32,48,2560]{2,1,0:T(8,128)(2,1)}), bf16[32,48,2560]{2,1,0:T(8,128)(2,1)}, u32[]{:S(2)}, u32[]{:S(2)}) async-start(bf16[32,48,2560]{2,1,0:T(8,128)(2,1)} %bitcast.195), calls=%async_computation | async-start | bytes 15728640 | tf_op jit(solution)/shard_map/all_to_all | solution.py:84
  320.1 3.8 collective-permute-start.38
  323.9 15.7 %collective-permute-start.39 = (f32[8,1536]{1,0:T(8,128)S(1)}, f32[8,1536]{1,0:T(8,128)S(1)}, u32[]{:S(2)}, u32[]{:S(2)}) collective-permute-start(f32[8,1536]{1,0:T(8,128)S(1)} %fusion.140), channel_id=1, source_target_pairs={{0,16},{2,18},{4,20},{6,22},{8,24},{10,26},{12,28},{14,30},{16,0},... | collective-permute-start | bytes 147464 | tf_op jit(solution)/shard_map/ppermute | solution.py:42
  339.6 43.5 %collective-permute-start.41 = (f32[8,1536]{1,0:T(8,128)S(1)}, f32[8,1536]{1,0:T(8,128)S(1)}, u32[]{:S(2)}, u32[]{:S(2)}) collective-permute-start(f32[8,1536]{1,0:T(8,128)S(1)} %add.439), channel_id=1, source_target_pairs={{0,4},{2,6},{4,8},{6,10},{8,12},{10,14},{12,0},{14,2},{16,20},{18,... | collective-permute-start | bytes 147464 | tf_op jit(solution)/shard_map/ppermute | solution.py:42
  349.4 39.5 %collective-permute-start.42 = (f32[8,1536]{1,0:T(8,128)S(1)}, f32[8,1536]{1,0:T(8,128)S(1)}, u32[]{:S(2)}, u32[]{:S(2)}) collective-permute-start(f32[8,1536]{1,0:T(8,128)S(1)} %add.439), channel_id=1, source_target_pairs={{0,12},{2,14},{4,0},{6,2},{8,4},{10,6},{12,8},{14,10},{16,28},{18,... | collective-permute-start | bytes 147464 | tf_op jit(solution)/shard_map/ppermute | solution.py:42
  380.2 18.4 %collective-permute-start.40 = (f32[8,1536]{1,0:T(8,128)S(1)}, f32[8,1536]{1,0:T(8,128)S(1)}, u32[]{:S(2)}, u32[]{:S(2)}) collective-permute-start(f32[8,1536]{1,0:T(8,128)S(1)} %add.439), channel_id=1, source_target_pairs={{0,8},{2,10},{4,12},{6,14},{8,0},{10,2},{12,4},{14,6},{16,24},{18,... | collective-permute-start | bytes 147464 | tf_op jit(solution)/shard_map/ppermute | solution.py:42
  382.8 88.8 %collective-permute-start.35 = (bf16[256,1536]{1,0:T(8,128)(2,1)}, bf16[256,1536]{1,0:T(8,128)(2,1)}, u32[]{:S(2)}, u32[]{:S(2)}) collective-permute-start(bf16[256,1536]{1,0:T(8,128)(2,1)} %constant_dynamic-slice_fusion.2), channel_id=1, source_target_pairs={{0,1},{1,0},{2,3},{3,2},{4,5},{5,4},{6,7},{7,6},{8,9},{9,8},{10,11... | collective-permute-start | bytes 2359304 | tf_op jit(solution)/shard_map/ppermute | solution.py:46
  398.6 45.9 %collective-permute-start.44 = (f32[8,1536]{1,0:T(8,128)S(1)}, f32[8,1536]{1,0:T(8,128)S(1)}, u32[]{:S(2)}, u32[]{:S(2)}) collective-permute-start(f32[8,1536]{1,0:T(8,128)S(1)} %add_add_fusion.1), channel_id=1, source_target_pairs={{0,32},{2,34},{4,36},{6,38},{8,40},{10,42},{12,44},{14,46},{16,48}... | collective-permute-start | bytes 147464 | tf_op jit(solution)/shard_map/ppermute | solution.py:42
  404.0 40.5 %collective-permute-start.45 = (f32[8,1536]{1,0:T(8,128)S(1)}, f32[8,1536]{1,0:T(8,128)S(1)}, u32[]{:S(2)}, u32[]{:S(2)}) collective-permute-start(f32[8,1536]{1,0:T(8,128)S(1)} %add_add_fusion.1), channel_id=1, source_target_pairs={{0,96},{2,98},{4,100},{6,102},{8,104},{10,106},{12,108},{14,110},{... | collective-permute-start | bytes 147464 | tf_op jit(solution)/shard_map/ppermute | solution.py:42
  408.2 48.3 %collective-permute-start.43 = (f32[8,1536]{1,0:T(8,128)S(1)}, f32[8,1536]{1,0:T(8,128)S(1)}, u32[]{:S(2)}, u32[]{:S(2)}) collective-permute-start(f32[8,1536]{1,0:T(8,128)S(1)} %add_add_fusion.1), channel_id=1, source_target_pairs={{0,64},{2,66},{4,68},{6,70},{8,72},{10,74},{12,76},{14,78},{16,80}... | collective-permute-start | bytes 147464 | tf_op jit(solution)/shard_map/ppermute | solution.py:42
  410.3 52.6 %collective-permute-start.37 = (bf16[256,1536]{1,0:T(8,128)(2,1)}, bf16[256,1536]{1,0:T(8,128)(2,1)S(1)}, u32[]{:S(2)}, u32[]{:S(2)}) collective-permute-start(bf16[256,1536]{1,0:T(8,128)(2,1)} %constant_dynamic-slice_fusion.1), channel_id=1, source_target_pairs={{0,1},{1,0},{2,3},{3,2},{4,5},{5,4},{6,7},{7,6},{8,9},{9,8},{10,11... | collective-permute-start | bytes 2359304 | tf_op jit(solution)/shard_map/ppermute | solution.py:46
  469.0 6.2 %collective-permute-start.48 = (f32[24,2560]{1,0:T(8,128)S(1)}, f32[24,2560]{1,0:T(8,128)S(1)}, u32[]{:S(2)}, u32[]{:S(2)}) collective-permute-start(f32[24,2560]{1,0:T(8,128)S(1)} %constant_dynamic-slice_fusion), channel_id=1, source_target_pairs={{0,2},{2,0},{4,6},{6,4},{8,10},{10,8},{12,14},{14,12},{16,18},{18,... | collective-permute-start | bytes 737288 | tf_op jit(solution)/shard_map/ppermute | solution.py:42
  (81 other events, 845.0 us)
